TPU v7x, 128 devices: a whole 4x4x4 slice. The times are simulated.
128 devices in a mesh: lat: 64 (over z, y, x), obs: 2 (over core).
Axes of the slice: x: 4, y: 4, z: 4, core: 2. Of those that a mesh axis runs over, the one named last changes fastest.
Arguments:
- control: bfloat16 [2, 64, 512, 3072], P(None, 'obs', 'lat'), may hold values from -8 to 8
- zonal_scales: float32 [4], replicated, may hold values from 1.5 to 360, as said below
- zonal_heights: float32 [4], replicated, may hold values from 0.25 to 0.75
- meridional_scales: float32 [4], replicated, may hold values from 0.8 to 180, as said below
- meridional_heights: float32 [4], replicated, may hold values from 0.25 to 0.75
- vertical_map: bfloat16 [2, 64, 64], replicated, may hold values from -0.75 to 0.75
- send_blocks: int32 [64, 2, 2, 2], P('lat', 'obs'), may hold values from 0 to 63
- report_slot: int32 [64, 2, 2048], P('lat', 'obs'), may hold values from 0 to 3
- report_level: int32 [64, 2, 2048], P('lat', 'obs'), may hold values from 0 to 127
- report_corner: int32 [64, 2, 4, 2048], P('lat', 'obs'), may hold values from 0 to 191, as said below
- report_weight: float32 [64, 2, 4, 2048], P('lat', 'obs'), may hold values from 0 to 1, as said below
- innovation: float32 [64, 2, 2048], P('lat', 'obs'), may hold values from -6 to 6
- report_precision: float32 [64, 2, 2048], P('lat', 'obs'), may hold values from 1 to 4
Outputs:
- weighted_departure: float32 [64, 2, 2048], P('lat', 'obs')
- control_gradient: float32 [2, 64, 512, 3072], P(None, 'obs', 'lat')
Inputs may be any that keep to these rules, and one draw needn't show every extreme that they name: `report_corner`: the corners of an observation are q, q + 1, q + 48, q + 49 in this order, with q // 48 < 3 and q % 48 < 47. `report_weight`: nonnegative bilinear weights whose four values sum to one, in the corner order of report_corner. `zonal_scales`: positive length scales. `meridional_scales`: positive length scales.
All inputs are finite; a program needn't handle non-finite values.
Results may differ from a plain program's by a relative error of at most 0.009.
Values may be sent and summed in bfloat16 or wider, within the bound.
No kernel may reach another device: no remote copies, remote signals or barrier semaphores. Data moves between devices by JAX's collectives and lax.ppermute only.
A program may use at most 128 MiB of HBM per device.

v0:
```python
import math

import jax
import jax.numpy as jnp
from jax import lax
from jax.sharding import PartitionSpec as P

SLOTS = 2
BR = 4


def profile(distance, scales, heights):
    total = jnp.zeros(distance.shape, jnp.float32)
    for member in range(4):
        scale = scales[member]
        total = total + heights[member] * jnp.exp(
            -distance * distance / (2.0 * scale * scale)
        ) / jnp.sqrt(math.sqrt(math.pi) * scale)
    return total


def zonal_apply(source, pattern, out_shape, out_type, scales, heights):
    width = out_shape[-1]
    stride = math.gcd(width, 512)
    result = jnp.zeros(out_shape, out_type)
    column_ids = jnp.arange(width)[:, None]

    def one_block(counter, acc_field):
        start = counter * stride
        target = start + jnp.arange(stride)[None, :]
        offset = jnp.abs(column_ids - target)
        distance = jnp.minimum(offset, width - offset).astype(jnp.float32)
        kernel = profile(distance, scales, heights).astype(jnp.bfloat16)
        part_out = jnp.einsum(pattern, source, kernel, preferred_element_type=jnp.float32).astype(
            out_type
        )
        return lax.dynamic_update_slice_in_dim(acc_field, part_out, start, len(out_shape) - 1)

    return lax.fori_loop(0, width // stride, one_block, result)


def on_device(
    control,
    zonal_scales,
    zonal_heights,
    meridional_scales,
    meridional_heights,
    vertical_map,
    send_blocks,
    report_slot,
    report_level,
    report_corner,
    report_weight,
    innovation,
    report_precision,
):
    lat_count = lax.axis_size("lat")
    owner_count = lax.axis_size("obs")
    variables, level_share, band_rows, width = control.shape
    strip = width // lat_count
    all_rows = band_rows * lat_count
    levels = level_share * owner_count
    column_rows = all_rows // owner_count
    block_count = column_rows // BR
    slot_count = owner_count * SLOTS
    places = jnp.arange(all_rows)
    apart = jnp.abs(places[:, None] - places[None, :]).astype(jnp.float32)
    meridional = profile(apart, meridional_scales, meridional_heights).astype(jnp.bfloat16)
    smoothed = zonal_apply(
        control,
        "vlyx,xz->vylz",
        (variables, band_rows, level_share, width),
        jnp.bfloat16,
        zonal_scales,
        zonal_heights,
    )
    smoothed = smoothed.reshape(variables, band_rows, level_share, lat_count, strip)
    lines = lax.all_to_all(smoothed, "lat", split_axis=3, concat_axis=1, tiled=True)
    items = lines.shape[0]
    flat = lines.reshape(items, all_rows, level_share * strip)
    mixed = jnp.einsum("ay,vyc->vac", meridional, flat, preferred_element_type=jnp.float32).astype(
        jnp.bfloat16
    )
    lined = mixed.reshape(items, all_rows, level_share, strip)
    columns = lax.all_to_all(lined, "obs", split_axis=1, concat_axis=2, tiled=True)
    increment = jnp.einsum(
        "vlk,vykx->vylx", vertical_map, columns, preferred_element_type=jnp.float32
    )
    sends = send_blocks.reshape(slot_count)
    blocks = increment.reshape(variables, block_count, BR, levels, strip)
    selector = (sends[:, None] == jnp.arange(block_count)[None, :]).astype(jnp.float32)
    outgoing = jnp.einsum("sb,vbrlx->vsrlx", selector, blocks, precision=lax.Precision.HIGHEST)
    incoming = lax.all_to_all(
        outgoing.astype(jnp.bfloat16), "obs", split_axis=1, concat_axis=1, tiled=True
    ).astype(outgoing.dtype)
    slot = report_slot.reshape(1, -1)
    level_code = report_level.reshape(1, -1)
    corner = report_corner.reshape(4, -1)
    position = (
        ((level_code // levels * slot_count + slot) * BR + corner // strip) * levels
        + level_code % levels
    ) * strip + corner % strip
    values = jnp.take(incoming.reshape(-1), position)
    stencil = report_weight.reshape(4, -1)
    model_value = jnp.sum(stencil * values, axis=0).reshape(report_slot.shape)
    departure = report_precision * (model_value - innovation)
    pushes = stencil * departure.reshape(1, -1)
    spread = (
        jnp.zeros((incoming.size,), jnp.float32).at[position.reshape(-1)].add(pushes.reshape(-1))
    )
    returned = lax.all_to_all(
        spread.reshape(incoming.shape).astype(jnp.bfloat16),
        "obs",
        split_axis=1,
        concat_axis=1,
        tiled=True,
    ).astype(jnp.float32)
    adjoint = jnp.einsum(
        "sb,vsrlx->vbrlx", selector, returned, precision=lax.Precision.HIGHEST
    ).reshape(increment.shape)
    lifted = jnp.einsum(
        "vlk,vylx->vykx", vertical_map.astype(jnp.float32), adjoint, precision=lax.Precision.HIGHEST
    ).astype(jnp.bfloat16)
    lines = lax.all_to_all(lifted, "obs", split_axis=2, concat_axis=1, tiled=True)
    items = lines.shape[0]
    flat = lines.reshape(items, all_rows, level_share * strip)
    mixed = jnp.einsum("ya,vyc->vac", meridional, flat, preferred_element_type=jnp.float32).astype(
        jnp.bfloat16
    )
    returned_lines = mixed.reshape(items, all_rows, level_share, 1, strip)
    lines = lax.all_to_all(returned_lines, "lat", split_axis=1, concat_axis=3, tiled=True)
    items = lines.shape[0]
    flat = lines.reshape(items, band_rows, level_share, width)
    gradient = zonal_apply(
        flat,
        "vylx,xz->vlyz",
        (items, level_share, band_rows, width),
        jnp.float32,
        zonal_scales,
        zonal_heights,
    )
    return (departure, gradient)


def solution(mesh):
    in_specs = (
        P(None, "obs", "lat", None),
        P(),
        P(),
        P(),
        P(),
        P(),
        P("lat", "obs", None, None),
        P("lat", "obs", None),
        P("lat", "obs", None),
        P("lat", "obs", None, None),
        P("lat", "obs", None, None),
        P("lat", "obs", None),
        P("lat", "obs", None),
    )
    out_specs = (P("lat", "obs", None), P(None, "obs", "lat", None))
    return jax.shard_map(
        on_device, mesh=mesh, in_specs=in_specs, out_specs=out_specs, check_vma=False
    )
```

profile of v0, /device:TPU:0, one launch (start us, length us, event | category | flops | bytes accessed | tf_op | source)
XLA Modules:
  0.0 705.5 jit_solution(15430325345000851225)
XLA Ops:
  15.6 81.6 %while.32 = (s32[]{:T(128)}, bf16[2,8,32,3072]{3,2,1,0:T(8,128)(2,1)S(1)}, f32[4]{0:T(128)S(1)}, f32[]{:T(128)}, f32[]{:T(128)}, /*index=5*/f32[]{:T(128)}, f32[...) while((s32[]{:T(128)}, ...), condition=%wide.region_1.0_spmd.clone, body=%wide.region_0.0_spmd.clone.sunk | while | flops 1647051264 | bytes 3674395 | solution.py:39
  16.2 12.9 %fusion.170 = bf16[2,8,32,3072]{3,2,1,0:T(8,128)(2,1)S(1)} fusion(bf16[2,8,32,3072]{3,2,1,0:T(8,128)(2,1)S(1)} %get-tuple-element.735, s32[]{:T(128)S(6)} %select_n.204, bf16[2,32,8,3072]{3,1,2,0:T(8,128)(2,1)} %get-tuple-element.761, f32[]{:T(128)} %get-tuple-element.760, f32[]{:T(128)} %get-tuple-element.759, f32[]{:T(128)} %bitcast.231, ...), kind=kOutput, calls=%fused_computation.47.clone.1 | convolution fusion | flops 1647050752 | bytes 3672116 | tf_op jit(solution)/shard_map/while/body/eval_jaxpr/vlyx,xz->vylz/dot_general | solution.py:34
  29.8 12.9 %fusion.170 = bf16[2,8,32,3072]{3,2,1,0:T(8,128)(2,1)S(1)} fusion(bf16[2,8,32,3072]{3,2,1,0:T(8,128)(2,1)S(1)} %get-tuple-element.735, s32[]{:T(128)S(6)} %select_n.204, bf16[2,32,8,3072]{3,1,2,0:T(8,128)(2,1)} %get-tuple-element.761, f32[]{:T(128)} %get-tuple-element.760, f32[]{:T(128)} %get-tuple-element.759, f32[]{:T(128)} %bitcast.231, ...), kind=kOutput, calls=%fused_computation.47.clone.1 | convolution fusion | flops 1647050752 | bytes 3672116 | tf_op jit(solution)/shard_map/while/body/eval_jaxpr/vlyx,xz->vylz/dot_general | solution.py:34
  43.4 12.9 %fusion.170 = bf16[2,8,32,3072]{3,2,1,0:T(8,128)(2,1)S(1)} fusion(bf16[2,8,32,3072]{3,2,1,0:T(8,128)(2,1)S(1)} %get-tuple-element.735, s32[]{:T(128)S(6)} %select_n.204, bf16[2,32,8,3072]{3,1,2,0:T(8,128)(2,1)} %get-tuple-element.761, f32[]{:T(128)} %get-tuple-element.760, f32[]{:T(128)} %get-tuple-element.759, f32[]{:T(128)} %bitcast.231, ...), kind=kOutput, calls=%fused_computation.47.clone.1 | convolution fusion | flops 1647050752 | bytes 3672116 | tf_op jit(solution)/shard_map/while/body/eval_jaxpr/vlyx,xz->vylz/dot_general | solution.py:34
  57.0 12.9 %fusion.170 = bf16[2,8,32,3072]{3,2,1,0:T(8,128)(2,1)S(1)} fusion(bf16[2,8,32,3072]{3,2,1,0:T(8,128)(2,1)S(1)} %get-tuple-element.735, s32[]{:T(128)S(6)} %select_n.204, bf16[2,32,8,3072]{3,1,2,0:T(8,128)(2,1)} %get-tuple-element.761, f32[]{:T(128)} %get-tuple-element.760, f32[]{:T(128)} %get-tuple-element.759, f32[]{:T(128)} %bitcast.231, ...), kind=kOutput, calls=%fused_computation.47.clone.1 | convolution fusion | flops 1647050752 | bytes 3672116 | tf_op jit(solution)/shard_map/while/body/eval_jaxpr/vlyx,xz->vylz/dot_general | solution.py:34
  70.6 12.9 %fusion.170 = bf16[2,8,32,3072]{3,2,1,0:T(8,128)(2,1)S(1)} fusion(bf16[2,8,32,3072]{3,2,1,0:T(8,128)(2,1)S(1)} %get-tuple-element.735, s32[]{:T(128)S(6)} %select_n.204, bf16[2,32,8,3072]{3,1,2,0:T(8,128)(2,1)} %get-tuple-element.761, f32[]{:T(128)} %get-tuple-element.760, f32[]{:T(128)} %get-tuple-element.759, f32[]{:T(128)} %bitcast.231, ...), kind=kOutput, calls=%fused_computation.47.clone.1 | convolution fusion | flops 1647050752 | bytes 3672116 | tf_op jit(solution)/shard_map/while/body/eval_jaxpr/vlyx,xz->vylz/dot_general | solution.py:34
  84.2 12.9 %fusion.170 = bf16[2,8,32,3072]{3,2,1,0:T(8,128)(2,1)S(1)} fusion(bf16[2,8,32,3072]{3,2,1,0:T(8,128)(2,1)S(1)} %get-tuple-element.735, s32[]{:T(128)S(6)} %select_n.204, bf16[2,32,8,3072]{3,1,2,0:T(8,128)(2,1)} %get-tuple-element.761, f32[]{:T(128)} %get-tuple-element.760, f32[]{:T(128)} %get-tuple-element.759, f32[]{:T(128)} %bitcast.231, ...), kind=kOutput, calls=%fused_computation.47.clone.1 | convolution fusion | flops 1647050752 | bytes 3672116 | tf_op jit(solution)/shard_map/while/body/eval_jaxpr/vlyx,xz->vylz/dot_general | solution.py:34
  106.8 12.0 %copy.95 = bf16[2,8,32,64,48]{4,2,1,0,3:T(8,128)(2,1)} copy(bf16[2,8,32,64,48]{4,3,2,1,0:T(8,128)(2,1)} %reshape.424) | data formatting | bytes 6291456 | tf_op jit(solution)/shard_map/reshape | solution.py:77
  118.9 18.7 %reshape.463 = bf16[64,2,12288]{2,1,0:T(2,128)(2,1)} reshape(bf16[64,2,8,32,48]{4,3,2,1,0:T(8,128)(2,1)} %bitcast.244) | data formatting | bytes 6291456
  137.6 11.6 %all-to-all-start = ((bf16[64,2,12288]{2,1,0:T(2,128)(2,1)}), bf16[64,2,12288]{2,1,0:T(2,128)(2,1)S(1)}, u32[]{:S(2)}, u32[]{:S(2)}) async-start(bf16[64,2,12288]{2,1,0:T(2,128)(2,1)} %reshape.463), calls=%async_computation | async-start | bytes 6291456 | tf_op jit(solution)/shard_map/all_to_all | solution.py:78
  159.1 31.7 %all-to-all-done = bf16[64,2,12288]{2,1,0:T(2,128)(2,1)S(1)} async-done(((bf16[64,2,12288]{2,1,0:T(2,128)(2,1)}), bf16[64,2,12288]{2,1,0:T(2,128)(2,1)S(1)}, u32[]{:S(2)}, u32[]{:S(2)}) %all-to-all-start) | async-done | bytes 3145760 | tf_op jit(solution)/shard_map/all_to_all | solution.py:78
  219.6 14.9 %reshape.425 = bf16[2,512,1536]{2,1,0:T(8,128)(2,1)S(1)} reshape(bf16[2,64,8,32,1,48]{5,3,2,1,0,4:T(8,128)(2,1)} %copy.40) | data formatting | bytes 6291456 | tf_op jit(solution)/shard_map/reshape | solution.py:80
  241.1 12.6 %copy.42 = bf16[2,512,32,48]{3,2,0,1:T(8,128)(2,1)} copy(bf16[2,512,32,48]{1,3,2,0:T(8,128)(2,1)} %bitcast.254) | data formatting | bytes 6291456 | tf_op jit(solution)/shard_map/reshape | solution.py:84
  253.7 14.9 %reshape.465 = bf16[2,2,393216]{2,1,0:T(2,128)(2,1)S(1)} reshape(bf16[512,2,32,48]{3,2,1,0:T(8,128)(2,1)} %bitcast.245) | data formatting | bytes 6291456
  287.3 11.9 %copy.43 = bf16[2,2,256,32,48]{2,3,1,4,0:T(8,128)(2,1)S(1)} copy(bf16[2,2,256,32,48]{4,3,0,2,1:T(8,128)(2,1)} %bitcast.246) | data formatting | bytes 6291456 | tf_op jit(solution)/shard_map/all_to_all | solution.py:85
  314.3 15.5 %fusion.105 = bf16[2,4,4,64,48]{3,1,4,2,0:T(4,128)(2,1)S(1)} fusion(f32[2,64,4,64,48]{3,4,2,1,0:T(8,128)} %bitcast.242, s32[4]{0:T(128)S(1)} %eq.19), kind=kOutput, calls=%fused_computation.107 | convolution fusion | flops 75596032 | bytes 6488080 | tf_op jit(solution)/shard_map/sb,vbrlx->vsrlx/dot_general | solution.py:92
  335.2 45.5 %gather_fusion = f32[8192]{0:T(1024)S(1)} fusion(f32[98304]{0:T(1024)S(1)} %reshape.437, s32[8192]{0:T(1024)S(1)} %broadcast_clamp_fusion), kind=kCustom, calls=%fused_computation | custom fusion | bytes 98304 | tf_op jit(solution)/shard_map/jit(_take)/gather | solution.py:103
  381.6 43.3 %scatter_custom_fusion = f32[98304]{0:T(1024)S(1)} fusion(s32[8192]{0:T(1024)S(1)} %bitcast.269, f32[8192]{0:T(1024)S(1)} %mul.590, f32[]{:T(128)} %constant.182.clone.1), kind=kCustom, calls=%fused_computation.117 | custom fusion | flops 8192 | bytes 393220 | tf_op jit(solution)/shard_map/scatter-add | solution.py:109
  436.0 13.4 %copy.50 = f32[2,64,4,64,48]{3,4,2,1,0:T(8,128)} copy(f32[2,64,4,64,48]{1,3,4,2,0:T(8,128)} %convolution_bitcast_fusion) | data formatting | bytes 12582912 | tf_op jit(solution)/shard_map/sb,vsrlx->vbrlx/transpose | solution.py:118
  449.4 15.4 %convert_bitcast_fusion = bf16[2,256,64,48]{1,2,3,0:T(8,128)(2,1)S(1)} fusion(f32[2,256,64,48]{2,3,1,0:T(8,128)} %bitcast.243, bf16[2,64,64]{2,1,0:T(8,128)(2,1)S(1)} %copy-done), kind=kOutput, calls=%fused_computation.103 | convolution fusion | flops 1209532416 | bytes 9453568 | tf_op jit(solution)/shard_map/vlk,vylx->vykx/dot_general | solution.py:121
  486.8 12.2 %copy.55 = bf16[2,512,32,1,48]{4,2,0,3,1:T(8,128)(2,1)} copy(bf16[2,512,32,1,48]{1,4,2,0,3:T(8,128)(2,1)S(1)} %bitcast.253) | data formatting | bytes 6291456 | tf_op jit(solution)/shard_map/reshape | solution.py:130
  499.0 18.3 %reshape.471 = bf16[64,2,12288]{2,1,0:T(2,128)(2,1)} reshape(bf16[512,1,2,32,48]{4,3,2,1,0:T(8,128)(2,1)} %bitcast.247) | data formatting | bytes 6291456
  524.6 42.0 %all-to-all-done.5 = bf16[64,2,12288]{2,1,0:T(2,128)(2,1)S(1)} async-done(((bf16[64,2,12288]{2,1,0:T(2,128)(2,1)}), bf16[64,2,12288]{2,1,0:T(2,128)(2,1)S(1)}, u32[]{:S(2)}, u32[]{:S(2)}) %all-to-all-start.5) | async-done | bytes 3145760 | tf_op jit(solution)/shard_map/all_to_all | solution.py:131
  584.1 12.1 %copy.57 = bf16[2,8,32,64,1,48]{5,3,2,1,0,4:T(8,128)(2,1)} copy(bf16[2,8,32,64,1,48]{5,2,1,3,0,4:T(8,128)(2,1)} %bitcast.249) | data formatting | bytes 6291456 | tf_op jit(solution)/shard_map/all_to_all | solution.py:131
  596.2 15.7 %reshape.435 = bf16[2,8,32,3072]{3,2,1,0:T(8,128)(2,1)} reshape(bf16[2,8,32,64,1,48]{5,3,2,1,0,4:T(8,128)(2,1)} %copy.57) | data formatting | bytes 6291456 | tf_op jit(solution)/shard_map/reshape | solution.py:133
  615.4 89.2 %while.33 = (s32[]{:T(128)}, f32[2,32,8,3072]{3,2,1,0:T(8,128)}, f32[4]{0:T(128)S(1)}, f32[]{:T(128)}, f32[]{:T(128)}, /*index=5*/f32[]{:T(128)}, f32[]{:T(128)}...) while((s32[]{:T(128)}, f32[2,32,8,3072]{3,2,1,0:T(8,128)}, ...), condition=%wide.region_5.6_spmd.clone, body=%wide.region_4.5_spmd.clone.sunk | while | flops 1646789120 | bytes 6295835 | solution.py:39
  616.2 12.6 %fusion.174 = f32[2,32,8,512]{3,1,2,0:T(8,128)S(1)} fusion(bf16[2,8,32,3072]{3,2,1,0:T(8,128)(2,1)} %get-tuple-element.809, f32[]{:T(128)} %get-tuple-element.808, f32[]{:T(128)} %get-tuple-element.807, f32[]{:T(128)} %bitcast.238, f32[]{:T(128)} %get-tuple-element.806, f32[]{:T(128)} %get-tuple-element.805, f32[]{:T(128)} %bitcast.239, ...), kind=kOutput, calls=%fused_computation.91.clone.1 | convolution fusion | flops 1646788608 | bytes 4196400 | tf_op jit(solution)/shard_map/while/body/eval_jaxpr/vylx,xz->vlyz/dot_general | solution.py:34
  631.0 12.6 %fusion.174 = f32[2,32,8,512]{3,1,2,0:T(8,128)S(1)} fusion(bf16[2,8,32,3072]{3,2,1,0:T(8,128)(2,1)} %get-tuple-element.809, f32[]{:T(128)} %get-tuple-element.808, f32[]{:T(128)} %get-tuple-element.807, f32[]{:T(128)} %bitcast.238, f32[]{:T(128)} %get-tuple-element.806, f32[]{:T(128)} %get-tuple-element.805, f32[]{:T(128)} %bitcast.239, ...), kind=kOutput, calls=%fused_computation.91.clone.1 | convolution fusion | flops 1646788608 | bytes 4196400 | tf_op jit(solution)/shard_map/while/body/eval_jaxpr/vylx,xz->vlyz/dot_general | solution.py:34
  645.8 12.6 %fusion.174 = f32[2,32,8,512]{3,1,2,0:T(8,128)S(1)} fusion(bf16[2,8,32,3072]{3,2,1,0:T(8,128)(2,1)} %get-tuple-element.809, f32[]{:T(128)} %get-tuple-element.808, f32[]{:T(128)} %get-tuple-element.807, f32[]{:T(128)} %bitcast.238, f32[]{:T(128)} %get-tuple-element.806, f32[]{:T(128)} %get-tuple-element.805, f32[]{:T(128)} %bitcast.239, ...), kind=kOutput, calls=%fused_computation.91.clone.1 | convolution fusion | flops 1646788608 | bytes 4196400 | tf_op jit(solution)/shard_map/while/body/eval_jaxpr/vylx,xz->vlyz/dot_general | solution.py:34
  660.7 12.6 %fusion.174 = f32[2,32,8,512]{3,1,2,0:T(8,128)S(1)} fusion(bf16[2,8,32,3072]{3,2,1,0:T(8,128)(2,1)} %get-tuple-element.809, f32[]{:T(128)} %get-tuple-element.808, f32[]{:T(128)} %get-tuple-element.807, f32[]{:T(128)} %bitcast.238, f32[]{:T(128)} %get-tuple-element.806, f32[]{:T(128)} %get-tuple-element.805, f32[]{:T(128)} %bitcast.239, ...), kind=kOutput, calls=%fused_computation.91.clone.1 | convolution fusion | flops 1646788608 | bytes 4196400 | tf_op jit(solution)/shard_map/while/body/eval_jaxpr/vylx,xz->vlyz/dot_general | solution.py:34
  675.5 12.6 %fusion.174 = f32[2,32,8,512]{3,1,2,0:T(8,128)S(1)} fusion(bf16[2,8,32,3072]{3,2,1,0:T(8,128)(2,1)} %get-tuple-element.809, f32[]{:T(128)} %get-tuple-element.808, f32[]{:T(128)} %get-tuple-element.807, f32[]{:T(128)} %bitcast.238, f32[]{:T(128)} %get-tuple-element.806, f32[]{:T(128)} %get-tuple-element.805, f32[]{:T(128)} %bitcast.239, ...), kind=kOutput, calls=%fused_computation.91.clone.1 | convolution fusion | flops 1646788608 | bytes 4196400 | tf_op jit(solution)/shard_map/while/body/eval_jaxpr/vylx,xz->vlyz/dot_general | solution.py:34
  690.4 12.6 %fusion.174 = f32[2,32,8,512]{3,1,2,0:T(8,128)S(1)} fusion(bf16[2,8,32,3072]{3,2,1,0:T(8,128)(2,1)} %get-tuple-element.809, f32[]{:T(128)} %get-tuple-element.808, f32[]{:T(128)} %get-tuple-element.807, f32[]{:T(128)} %bitcast.238, f32[]{:T(128)} %get-tuple-element.806, f32[]{:T(128)} %get-tuple-element.805, f32[]{:T(128)} %bitcast.239, ...), kind=kOutput, calls=%fused_computation.91.clone.1 | convolution fusion | flops 1646788608 | bytes 4196400 | tf_op jit(solution)/shard_map/while/body/eval_jaxpr/vylx,xz->vlyz/dot_general | solution.py:34
  (113 shorter events, 173.3 us)
Async XLA Ops:
  0.6 298.6 %copy-start = (bf16[2,64,64]{2,1,0:T(8,128)(2,1)S(1)}, bf16[2,64,64]{2,1,0:T(8,128)(2,1)}, u32[]{:S(2)}) copy-start(bf16[2,64,64]{2,1,0:T(8,128)(2,1)} %param.22) | copy-start | bytes 49156
  0.6 14.9 %copy-start.2 = (f32[4]{0:T(128)S(1)}, f32[4]{0:T(128)}, u32[]{:S(2)}) copy-start(f32[4]{0:T(128)} %param.19) | copy-start | bytes 52
  118.8 30.4 %copy-start.8 = (s32[1,1,2048]{2,1,0:T(1,128)S(1)}, s32[1,1,2048]{2,1,0:T(1,128)}, u32[]{:S(2)}) copy-start(s32[1,1,2048]{2,1,0:T(1,128)} %param.24) | copy-start | bytes 24580
  118.8 30.4 %copy-start.9 = (s32[1,1,2048]{2,1,0:T(1,128)S(1)}, s32[1,1,2048]{2,1,0:T(1,128)}, u32[]{:S(2)}) copy-start(s32[1,1,2048]{2,1,0:T(1,128)} %param.25) | copy-start | bytes 24580
  118.8 30.5 %copy-start.3 = (s32[1,1,4,2048]{3,2,1,0:T(4,128)S(1)}, s32[1,1,4,2048]{3,2,1,0:T(4,128)}, u32[]{:S(2)}) copy-start(s32[1,1,4,2048]{3,2,1,0:T(4,128)} %param.26) | copy-start | bytes 98308
  118.8 30.6 %copy-start.6 = (f32[4]{0:T(128)S(1)}, f32[4]{0:T(128)}, u32[]{:S(2)}) copy-start(f32[4]{0:T(128)} %param.20) | copy-start | bytes 52
  118.8 39.0 %copy-start.12 = (s32[1,1,2,2]{3,2,1,0:T(2,128)S(1)}, s32[1,1,2,2]{3,2,1,0:T(2,128)}, u32[]{:S(2)}) copy-start(s32[1,1,2,2]{3,2,1,0:T(2,128)} %param.23) | copy-start | bytes 52
  118.9 39.1 %copy-start.4 = (f32[1,1,4,2048]{3,2,1,0:T(4,128)S(1)}, f32[1,1,4,2048]{3,2,1,0:T(4,128)}, u32[]{:S(2)}) copy-start(f32[1,1,4,2048]{3,2,1,0:T(4,128)} %param.27) | copy-start | bytes 98308
  137.6 20.6 %copy-start.7 = (f32[4]{0:T(128)S(1)}, f32[4]{0:T(128)}, u32[]{:S(2)}) copy-start(f32[4]{0:T(128)} %param.21) | copy-start | bytes 52
  137.6 53.2 %all-to-all-start = ((bf16[64,2,12288]{2,1,0:T(2,128)(2,1)}), bf16[64,2,12288]{2,1,0:T(2,128)(2,1)S(1)}, u32[]{:S(2)}, u32[]{:S(2)}) async-start(bf16[64,2,12288]{2,1,0:T(2,128)(2,1)} %reshape.463), calls=%async_computation | async-start | bytes 6291456 | tf_op jit(solution)/shard_map/all_to_all | solution.py:78
  335.2 45.7 %copy-start.10 = (f32[1,1,2048]{2,1,0:T(1,128)S(1)}, f32[1,1,2048]{2,1,0:T(1,128)}, u32[]{:S(2)}) copy-start(f32[1,1,2048]{2,1,0:T(1,128)} %param.29) | copy-start | bytes 24580
  335.2 45.7 %copy-start.11 = (f32[1,1,2048]{2,1,0:T(1,128)S(1)}, f32[1,1,2048]{2,1,0:T(1,128)}, u32[]{:S(2)}) copy-start(f32[1,1,2048]{2,1,0:T(1,128)} %param.28) | copy-start | bytes 24580
  381.0 0.6 copy-start.5
  517.2 49.4 %all-to-all-start.5 = ((bf16[64,2,12288]{2,1,0:T(2,128)(2,1)}), bf16[64,2,12288]{2,1,0:T(2,128)(2,1)S(1)}, u32[]{:S(2)}, u32[]{:S(2)}) async-start(bf16[64,2,12288]{2,1,0:T(2,128)(2,1)} %reshape.471), calls=%async_computation.5 | async-start | bytes 6291456 | tf_op jit(solution)/shard_map/all_to_all | solution.py:131
  704.6 0.8 copy-start.1
where the time goes:
time: 717 us; the launch traced here: 706 us
  local copies, waits for them, and re-layouts  323 us (45%)
  matrix products  207 us (29%)
  waiting for transfers between devices  73.8 us (10%)
  other arithmetic  43.8 us (6%)
  blocking collectives  21.5 us (3%)
  starting transfers between devices  19 us (3%)
  between operations  16.8 us (2%)
    dot_general x12, matrix products, one_block(): jnp.einsum(pattern, source, kernel, preferred_element_type=jnp.float32)  153 us
    unnamed x47, local copies, waits for them, and re-layouts  90.2 us
    gather x2, local copies, waits for them, and re-layouts, on_device(): values = jnp.take(incoming.reshape(-1), position)  45.6 us
    scatter-add x1, other arithmetic, on_device(): jnp.zeros((incoming.size,), jnp.float32).at[position.reshape(-1)]  43.3 us
    all_to_all x1, waiting for transfers between devices, on_device(): lax.all_to_all(returned_lines, 'lat', split_axis=1, concat_axis=3, tiled=...  42 us
    all_to_all x1, waiting for transfers between devices, on_device(): lax.all_to_all(smoothed, 'lat', split_axis=3, concat_axis=1, tiled=True)  31.7 us
    reshape x2, local copies, waits for them, and re-layouts, on_device(): smoothed.reshape(variables, band_rows, level_share, lat_count, strip)  21.7 us
    all_to_all x2, local copies, waits for them, and re-layouts, on_device(): lax.all_to_all(returned_lines, 'lat', split_axis=1, concat_axis=3, tiled=...  20.2 us
  transfers between devices with their start and end apart: 2, of which 2 were waited for; matrix products, arithmetic and copies ran while one was open for 0% of the time, Pallas kernels for 0%

commit v1 on v0

v1 whole, which is shorter than its diff:
```python
import math

import jax
import jax.numpy as jnp
from jax import lax
from jax.experimental import pallas as pl
from jax.experimental.pallas import tpu as pltpu
from jax.sharding import PartitionSpec as P

NV = 2
LH = 32
NX = 3072
NY = 512
XW = 48
BAND = 8
NLAT = 64
GROUP = 8 * XW
LANES = LH * XW
TILE = 256
SLAB = NX + 2 * TILE
WIDE = 3 * TILE
STEPS = NX // WIDE
ROWS = 16
COLS = ROWS * XW
REPORTS = 2048
MIB = 2**20

PIECES = (
    ((0, 48), (1, 96), (2, 128)),
    ((2, 16), (3, 64), (4, 112), (5, 128)),
    ((5, 32), (6, 80), (7, 128)),
)


def gaussians(distance, scales, heights):
    total = jnp.zeros(distance.shape, jnp.float32)
    for member in range(4):
        scale = scales[member]
        total = total + heights[member] * jnp.exp(
            -distance * distance / (2.0 * scale * scale)
        ) / jnp.sqrt(math.sqrt(math.pi) * scale)
    return total


def fill_slab(scales_ref, heights_ref, slab_ref):
    shape = (8, NX)
    offset = jnp.abs(
        lax.broadcasted_iota(jnp.int32, shape, 1) - lax.broadcasted_iota(jnp.int32, shape, 0)
    )
    distance = jnp.minimum(offset, NX - offset).astype(jnp.float32)
    scales = [jnp.full((1, 128), scales_ref[m], jnp.float32)[:, :1] for m in range(4)]
    heights = [jnp.full((1, 128), heights_ref[m], jnp.float32)[:, :1] for m in range(4)]
    base = gaussians(distance, scales, heights)
    for pair in range(TILE // 16):
        upper = base if pair == 0 else pltpu.roll(base, 16 * pair, 1)
        lower = pltpu.roll(base, 16 * pair + 8, 1)
        both = jnp.concatenate([upper, lower], axis=0).astype(jnp.bfloat16)
        slab_ref[16 * pair : 16 * pair + 16, :NX] = both
        slab_ref[16 * pair : 16 * pair + 16, NX:] = both[:, : SLAB - NX]


def zonal_columns(slab_ref, step):
    parts = []
    for block in range(NX // TILE):
        start = lax.rem(WIDE * step + (NX - TILE * block), NX)
        parts.append(slab_ref[:, pl.ds(pl.multiple_of(start, TILE), WIDE)])
    return jnp.concatenate(parts, axis=0)


def pick(tiles, shift, lane):
    result = []
    for tile, pieces in enumerate(PIECES):
        low = 128 * tile
        value = tiles[(pieces[-1][0] - shift) % 8][:, low : low + 128]
        for block, end in pieces[-2::-1]:
            value = jnp.where(lane < end, tiles[(block - shift) % 8][:, low : low + 128], value)
        result.append(value)
    return jnp.concatenate(result, axis=1)


def forward_zonal_kernel(scales_ref, heights_ref, field_ref, out_ref, slab_ref, acc_ref):
    step = pl.program_id(0)

    @pl.when(step == 0)
    def _():
        fill_slab(scales_ref, heights_ref, slab_ref)

    acc_ref[...] = jnp.dot(
        field_ref[...], zonal_columns(slab_ref, step), preferred_element_type=jnp.float32
    )
    lane = lax.broadcasted_iota(jnp.int32, (16, 128), 1)
    for strips in range(2):
        for group in range(LH // 8):
            turned = []
            for j in range(8):
                row = (group * 8 + j) * BAND
                both = jnp.concatenate(
                    [
                        acc_ref[v * LH * BAND + row : v * LH * BAND + row + BAND,
                                strips * GROUP : (strips + 1) * GROUP]
                        for v in range(NV)
                    ],
                    axis=0,
                )
                turned.append(both if j == 0 else pltpu.roll(both, XW * j, 1))
            for i in range(8):
                out_ref[strips * 8 + i, :, group * GROUP : (group + 1) * GROUP] = pick(
                    turned, i, lane
                ).astype(jnp.bfloat16)


def forward_zonal(field, scales, heights):
    return pl.pallas_call(
        forward_zonal_kernel,
        grid=(STEPS,),
        in_specs=[
            pl.BlockSpec(memory_space=pltpu.SMEM),
            pl.BlockSpec(memory_space=pltpu.SMEM),
            pl.BlockSpec((NV * LH * BAND, NX), lambda s: (0, 0)),
        ],
        out_specs=[
            pl.BlockSpec((NLAT // STEPS, 16, LANES), lambda s: (s, 0, 0)),
            pl.BlockSpec((TILE, SLAB), lambda s: (0, 0)),
        ],
        out_shape=[
            jax.ShapeDtypeStruct((NLAT, 16, LANES), jnp.bfloat16),
            jax.ShapeDtypeStruct((TILE, SLAB), jnp.bfloat16),
        ],
        scratch_shapes=[pltpu.VMEM((NV * LH * BAND, WIDE), jnp.float32)],
        compiler_params=pltpu.CompilerParams(vmem_limit_bytes=48 * MIB),
        cost_estimate=pl.CostEstimate(
            flops=2 * NV * LH * BAND * NX * NX, bytes_accessed=8 * MIB, transcendentals=10**5
        ),
        name="forward_zonal",
    )(scales, heights, field)


def backward_zonal_kernel(slab_ref, lines_ref, out_ref, field_ref):
    step = pl.program_id(0)

    @pl.when(step == 0)
    def _():
        lane = lax.broadcasted_iota(jnp.int32, (16, 128), 1)

        def fill(strips, carry):
            for group in range(LH // 8):
                tiles = [
                    lines_ref[strips * 8 + i, :, group * GROUP : (group + 1) * GROUP].astype(
                        jnp.float32
                    )
                    for i in range(8)
                ]
                for j in range(8):
                    level = pick(tiles, j, lane)
                    if j:
                        level = pltpu.roll(level, GROUP - XW * j, 1)
                    row = (group * 8 + j) * 16
                    start = pl.multiple_of(strips * GROUP, 128)
                    field_ref[row : row + 16, pl.ds(start, GROUP)] = level.astype(jnp.bfloat16)
            return carry

        lax.fori_loop(0, NLAT // 8, fill, 0)

    acc = jnp.dot(
        field_ref[...], zonal_columns(slab_ref, step), preferred_element_type=jnp.float32
    )
    for level in range(LH):
        for v in range(NV):
            row = (level * NV + v) * BAND
            out_ref[v, level] = acc[row : row + BAND]


def backward_zonal(slab, lines):
    return pl.pallas_call(
        backward_zonal_kernel,
        grid=(STEPS,),
        in_specs=[
            pl.BlockSpec((TILE, SLAB), lambda s: (0, 0)),
            pl.BlockSpec((NLAT, 16, LANES), lambda s: (0, 0, 0)),
        ],
        out_specs=pl.BlockSpec((NV, LH, BAND, WIDE), lambda s: (0, 0, 0, s)),
        out_shape=jax.ShapeDtypeStruct((NV, LH, BAND, NX), jnp.float32),
        scratch_shapes=[pltpu.VMEM((NV * LH * BAND, NX), jnp.bfloat16)],
        compiler_params=pltpu.CompilerParams(vmem_limit_bytes=48 * MIB),
        cost_estimate=pl.CostEstimate(
            flops=2 * NV * LH * BAND * NX * NX, bytes_accessed=12 * MIB, transcendentals=0
        ),
        name="backward_zonal",
    )(slab, lines)


def stencil_kernel(where_ref, mine_ref, other_ref, map_ref, stencil_ref, level_ref):
    strip_turn, half = where_ref[0], where_ref[1]
    shape = (LH, 2 * LH)
    slot = lax.broadcasted_iota(jnp.int32, shape, 0)
    level = (slot // 8) * 8 + lax.rem(lax.rem(slot, 8) + (8 - strip_turn), 8) + LH * half
    order = (lax.broadcasted_iota(jnp.int32, shape, 1) == level).astype(jnp.bfloat16)
    for owner, ref in enumerate((mine_ref, other_ref)):
        code = ref[1:2, :].astype(jnp.int32)
        for v in range(NV):
            rows = lax.broadcasted_iota(jnp.int32, (2 * LH, REPORTS), 0) + 2 * LH * v
            hot = (rows == code).astype(jnp.float32).astype(jnp.bfloat16)
            picked = lax.dot_general(
                map_ref[v], hot, (((0,), (0,)), ((), ())), preferred_element_type=jnp.float32
            ).astype(jnp.bfloat16)
            level_ref[owner, v * LH : (v + 1) * LH, :] = jnp.dot(
                order, picked, preferred_element_type=jnp.float32
            ).astype(jnp.bfloat16)
        base = ref[0:1, :] * float(4 * XW)
        points = [(base + ref[2 + c : 3 + c, :]).astype(jnp.int32) for c in range(4)]
        weights = [ref[6 + c : 7 + c, :] for c in range(4)]

        def fill(tile, carry):
            start = pl.multiple_of(tile * 16, 16)
            column = lax.broadcasted_iota(jnp.int32, (16, REPORTS), 0) + start
            value = jnp.zeros((16, REPORTS), jnp.float32)
            for c in range(4):
                value = jnp.where(column == points[c], weights[c], value)
            stencil_ref[owner, pl.ds(start, 16), :] = value.astype(jnp.bfloat16)
            return carry

        lax.fori_loop(0, COLS // 16, fill, 0)


def stencils(where, mine, other, vertical_map):
    return pl.pallas_call(
        stencil_kernel,
        in_specs=[pl.BlockSpec(memory_space=pltpu.SMEM)] + [pl.BlockSpec(memory_space=pltpu.VMEM)] * 3,
        out_shape=[
            jax.ShapeDtypeStruct((2, COLS, REPORTS), jnp.bfloat16),
            jax.ShapeDtypeStruct((2, NV * LH, REPORTS), jnp.bfloat16),
        ],
        compiler_params=pltpu.CompilerParams(vmem_limit_bytes=40 * MIB),
        cost_estimate=pl.CostEstimate(
            flops=10**8, bytes_accessed=8 * MIB, transcendentals=0
        ),
        name="stencils",
    )(where, mine, other, vertical_map)


def observe_kernel(rows_ref, lines_ref, stencil_ref, level_ref, out_ref, pick_ref, grid_ref):
    lines = lines_ref[...].reshape(NLAT * 16, LANES)
    mixed = jnp.dot(rows_ref[...], lines, preferred_element_type=jnp.float32)
    mixed = mixed.astype(jnp.bfloat16).astype(jnp.float32)
    for level in range(LH):
        pick_ref[level * 64 : (level + 1) * 64, :XW] = mixed[:, level * XW : (level + 1) * XW]
    for owner in range(2):
        for v in range(NV):
            for row in range(ROWS):
                start = (owner * NV + v) * ROWS + row
                column = owner * COLS + row * XW
                grid_ref[v * LH : (v + 1) * LH, column : column + XW] = pick_ref[
                    pl.ds(start, LH, stride=64), :
                ][:, :XW]
    for owner in range(2):
        points = grid_ref[:, owner * COLS : (owner + 1) * COLS].astype(jnp.bfloat16)
        columns = jnp.dot(points, stencil_ref[owner], preferred_element_type=jnp.float32)
        out_ref[owner : owner + 1, :] = jnp.sum(
            columns * level_ref[owner].astype(jnp.float32), axis=0, keepdims=True
        )


def observe(rows, lines, stencil, level):
    return pl.pallas_call(
        observe_kernel,
        out_shape=jax.ShapeDtypeStruct((2, REPORTS), jnp.float32),
        scratch_shapes=[
            pltpu.VMEM((LH * 64, 128), jnp.float32),
            pltpu.VMEM((NV * LH, 2 * COLS), jnp.float32),
        ],
        compiler_params=pltpu.CompilerParams(vmem_limit_bytes=48 * MIB),
        cost_estimate=pl.CostEstimate(
            flops=10**9, bytes_accessed=10 * MIB, transcendentals=0
        ),
        name="observe",
    )(rows, lines, stencil, level)


def spread_kernel(
    part_ref, peer_ref, mine_ref, other_ref, stencil_ref, level_ref, rows_ref,
    departure_ref, out_ref, pick_ref,
):
    for owner, ref in enumerate((mine_ref, other_ref)):
        value = part_ref[owner : owner + 1, :] + peer_ref[1 - owner : 2 - owner, :]
        departure = ref[11:12, :] * (value - ref[10:11, :])
        if owner == 0:
            departure_ref[...] = departure
        pushed = (level_ref[owner].astype(jnp.float32) * departure).astype(jnp.bfloat16)
        lifted = lax.dot_general(
            pushed, stencil_ref[owner], (((1,), (1,)), ((), ())), preferred_element_type=jnp.float32
        )
        lifted = jnp.concatenate([lifted, jnp.zeros((NV * LH, 128), jnp.float32)], axis=1)
        for v in range(NV):
            for row in range(ROWS):
                start = (owner * NV + v) * ROWS + row
                pick_ref[pl.ds(start, LH, stride=64), :] = lifted[
                    v * LH : (v + 1) * LH, row * XW : row * XW + 128
                ]
    parts = [pick_ref[level * 64 : (level + 1) * 64, :][:, :XW] for level in range(LH)]
    lines = jnp.concatenate(parts, axis=1).astype(jnp.bfloat16)
    out = jnp.dot(rows_ref[...], lines, preferred_element_type=jnp.float32)
    out_ref[...] = out.astype(jnp.bfloat16).reshape(NLAT, 16, LANES)


def spread(part, peer, mine, other, stencil, level, rows):
    return pl.pallas_call(
        spread_kernel,
        out_shape=[
            jax.ShapeDtypeStruct((1, REPORTS), jnp.float32),
            jax.ShapeDtypeStruct((NLAT, 16, LANES), jnp.bfloat16),
        ],
        scratch_shapes=[pltpu.VMEM((LH * 64, 128), jnp.float32)],
        compiler_params=pltpu.CompilerParams(vmem_limit_bytes=48 * MIB),
        cost_estimate=pl.CostEstimate(
            flops=10**9, bytes_accessed=10 * MIB, transcendentals=0
        ),
        name="spread",
    )(part, peer, mine, other, stencil, level, rows)


def on_device(
    control,
    zonal_scales,
    zonal_heights,
    meridional_scales,
    meridional_heights,
    vertical_map,
    send_blocks,
    report_slot,
    report_level,
    report_corner,
    report_weight,
    innovation,
    report_precision,
):
    strip = lax.axis_index("lat")
    half = lax.axis_index("obs")
    swap = [(0, 1), (1, 0)]

    mine = jnp.concatenate(
        [
            report_slot.reshape(1, -1).astype(jnp.float32),
            report_level.reshape(1, -1).astype(jnp.float32),
            report_corner.reshape(4, -1).astype(jnp.float32),
            report_weight.reshape(4, -1),
            innovation.reshape(1, -1),
            report_precision.reshape(1, -1),
        ],
        axis=0,
    )
    other = lax.ppermute(mine, "obs", swap)
    sends = send_blocks.reshape(2, 2)
    peer_sends = lax.ppermute(sends, "obs", swap)
    by_source = jnp.where(half == 0, jnp.stack([sends, peer_sends]), jnp.stack([peer_sends, sends]))
    by_owner = jnp.where(half == 0, by_source, by_source[:, ::-1]).transpose(1, 0, 2)
    anchor = jnp.arange(2).reshape(1, 2, 1, 1) * (NY // 2)
    rows = (anchor + by_owner[..., None] * 4 + jnp.arange(4)).reshape(2, 1, ROWS)
    rows = jnp.broadcast_to(rows, (2, NV, ROWS)).reshape(64)
    row_variable = (jnp.arange(64) // ROWS) % NV
    line = jnp.arange(NLAT * 16)
    line_row = (line // 16) * BAND + line % BAND
    line_variable = (line // BAND) % NV

    def meridional(a, av, b, bv):
        apart = jnp.abs(a - b).astype(jnp.float32)
        matrix = gaussians(apart, meridional_scales, meridional_heights)
        return jnp.where(av == bv, matrix, 0.0).astype(jnp.bfloat16)

    gather_rows = meridional(rows[:, None], row_variable[:, None], line_row[None], line_variable[None])
    spread_rows = meridional(line_row[:, None], line_variable[:, None], rows[None], row_variable[None])
    where = jnp.stack([strip % 8, half]).astype(jnp.int32)
    stencil, level = stencils(where, mine, other, vertical_map)

    smoothed, slab = forward_zonal(
        control.reshape(NV * LH * BAND, NX), zonal_scales, zonal_heights
    )
    lines = lax.all_to_all(smoothed, "lat", split_axis=0, concat_axis=0, tiled=True)
    part = observe(gather_rows, lines, stencil, level)
    peer = lax.ppermute(part, "obs", swap)
    departure, back = spread(part, peer, mine, other, stencil, level, spread_rows)
    back = lax.all_to_all(back, "lat", split_axis=0, concat_axis=0, tiled=True)
    gradient = backward_zonal(slab, back)
    return departure.reshape(report_slot.shape), gradient


def solution(mesh):
    in_specs = (
        P(None, "obs", "lat", None),
        P(),
        P(),
        P(),
        P(),
        P(),
        P("lat", "obs", None, None),
        P("lat", "obs", None),
        P("lat", "obs", None),
        P("lat", "obs", None, None),
        P("lat", "obs", None, None),
        P("lat", "obs", None),
        P("lat", "obs", None),
    )
    out_specs = (P("lat", "obs", None), P(None, "obs", "lat", None))
    return jax.shard_map(
        on_device, mesh=mesh, in_specs=in_specs, out_specs=out_specs, check_vma=False
    )
```

time: 717 us -> 151 us (0.21); the launches traced: 706 us -> 150 us
  local copies, waits for them, and re-layouts: 323 us -> 11.4 us
  matrix products: 207 us -> 0 us
  waiting for transfers between devices: 73.8 us -> 14.4 us
  Pallas kernels: 0 us -> 46.8 us
  other arithmetic: 43.8 us -> 7.66 us
  blocking collectives: 21.5 us -> 48.9 us
  between operations: 16.8 us -> 8.51 us
    dot_general x18 -> x0, matrix products: 207 us -> none  [the longest x12 153 us: one_block(): jnp.einsum(pattern, source, kernel, preferred_element_type=jnp.float32)]
    reshape x9 -> x0, local copies, waits for them, and re-layouts: 81.7 us -> none  [the longest x2 21.7 us: on_device(): smoothed.reshape(variables, band_rows, level_share, lat_count, strip)]
    unnamed x47 -> x38, local copies, waits for them, and re-layouts: 90.2 us -> 9.57 us
    all_to_all x2 -> x1, waiting for transfers between devices: 73.8 us -> 14.4 us  [on_device(): lax.all_to_all(smoothed, 'lat', split_axis=0, concat_axis=0, tiled=True)]
    all_to_all x6 -> x0, local copies, waits for them, and re-layouts: 54.9 us -> none  [the longest x2 20.2 us: on_device(): lax.all_to_all(returned_lines, 'lat', split_axis=1, concat_axis=3, tiled=...]
    pallas_call x0 -> x5, Pallas kernels: none -> 46.8 us  [the longest x1 13.9 us: forward_zonal(): pl.pallas_call(forward_zonal_kernel, grid=(STEPS,), in_specs=[pl.BlockSpe...]
    gather x2 -> x0, local copies, waits for them, and re-layouts: 45.6 us -> none  [on_device(): values = jnp.take(incoming.reshape(-1), position)]
    scatter-add x1 -> x0, other arithmetic: 43.3 us -> none  [on_device(): jnp.zeros((incoming.size,), jnp.float32).at[position.reshape(-1)]]
  transfers between devices with their start and end apart: 2 -> 4, of which waited for: 2 -> 1; matrix products, arithmetic and copies ran while one was open for 0% -> 6% of each run, Pallas kernels for 0% -> 6%
where the time goes in v1:
time: 151 us; the launch traced here: 150 us
  blocking collectives  48.9 us (32%)
  Pallas kernels  46.8 us (31%)
  waiting for transfers between devices  14.4 us (10%)
  starting transfers between devices  12.4 us (8%)
  local copies, waits for them, and re-layouts  11.4 us (8%)
  between operations  8.51 us (6%)
  other arithmetic  7.66 us (5%)
    all_to_all x1, blocking collectives, on_device(): back = lax.all_to_all(back, 'lat', split_axis=0, concat_axis=0, tiled=True)  48.9 us
    all_to_all x1, waiting for transfers between devices, on_device(): lax.all_to_all(smoothed, 'lat', split_axis=0, concat_axis=0, tiled=True)  14.4 us
    pallas_call x1, Pallas kernels, forward_zonal(): pl.pallas_call(forward_zonal_kernel, grid=(STEPS,), in_specs=[pl.BlockSpe...  13.9 us
    pallas_call x1, Pallas kernels, backward_zonal(): pl.pallas_call(backward_zonal_kernel, grid=(STEPS,), in_specs=[pl.BlockSp...  13.2 us
    all_to_all x1, starting transfers between devices, on_device(): lax.all_to_all(smoothed, 'lat', split_axis=0, concat_axis=0, tiled=True)  11.6 us
    unnamed x38, local copies, waits for them, and re-layouts  9.57 us
    pallas_call x1, Pallas kernels, stencils(): pl.pallas_call(stencil_kernel, in_specs=[pl.BlockSpec(memory_space=pltpu....  8.44 us
    convert_element_type x2, other arithmetic, meridional(): return jnp.where(av == bv, matrix, 0.0).astype(jnp.bfloat16)  6.96 us
  transfers between devices with their start and end apart: 4, of which 1 were waited for; matrix products, arithmetic and copies ran while one was open for 6% of the time, Pallas kernels for 6%

profile of v1, /device:TPU:0, one launch (start us, length us, event | category | flops | bytes accessed | tf_op | source)
XLA Modules:
  0.0 150.1 jit_solution(14732785151533338944)
XLA Ops:
  0.6 0.6 copy-done.5
  1.3 0.7 copy-done.6
  1.9 13.9 %forward_zonal.1 = (bf16[64,16,1536]{2,1,0:T(8,128)(2,1)S(1)}, bf16[256,3584]{1,0:T(8,128)(2,1)S(1)}) custom-call(f32[4]{0:T(128)S(1)} %copy-done.5, f32[4]{0:T(128)S(1)} %copy-done.6, bf16[512,3072]{1,0:T(8,128)(2,1)} %bitcast.34), custom_call_target="tpu_custom_call" | custom-call | flops 9663676416 | bytes 8388608 | tf_op jit(solution)/shard_map/forward_zonal/pallas_call | solution.py:113
  15.8 1.6 %copy-done.1 = bf16[64,16,1536]{2,1,0:T(8,128)(2,1)} copy-done((bf16[64,16,1536]{2,1,0:T(8,128)(2,1)}, bf16[64,16,1536]{2,1,0:T(8,128)(2,1)S(1)}, u32[]{:S(2)}) %copy-start.1) | copy-done | bytes 3145752
  17.4 1.3 copy-done.7
  18.7 0.0 copy-start.12
  18.8 11.6 %all-to-all-start = ((bf16[64,16,1536]{2,1,0:T(8,128)(2,1)}), bf16[64,16,1536]{2,1,0:T(8,128)(2,1)S(1)}, u32[]{:S(2)}, u32[]{:S(2)}) async-start(bf16[64,16,1536]{2,1,0:T(8,128)(2,1)} %copy-done.1), calls=%async_computation | async-start | bytes 6291456 | tf_op jit(solution)/shard_map/all_to_all | solution.py:377
  30.4 0.1 collective-permute-start
  30.6 0.2 concatenate.3.mine_ref
  30.8 0.6 collective-permute-start.1
  31.4 0.6 fusion.14
  39.6 0.1 add.151
  39.7 0.5 and_select_fusion
  40.2 0.1 pad_add_fusion.where_ref
  40.3 0.6 fusion.13
  41.0 0.1 add_bitcast_fusion
  41.1 0.1 add.148
  41.1 0.1 add.149
  41.2 0.1 sub.52
  41.3 3.5 %select_convert_fusion.1.rows_ref = bf16[64,1024]{1,0:T(8,128)(2,1)S(1)} fusion(f32[]{:T(128)S(6)} %sqrt.19, f32[]{:T(128)S(6)} %mul.156, f32[]{:T(128)} %bitcast.10, f32[]{:T(128)S(6)} %sqrt.18, f32[]{:T(128)S(6)} %mul.151, f32[]{:T(128)} %bitcast.8, f32[]{:T(128)S(6)} %sqrt.17, f32[]{:T(128)S(6)} %mul.146, f32[]{:T(128)} %bitcast.6, f32[]{:T(128)S(6)} %sqrt.16, ...), kind=kLoop, calls=%fused_computation.3 | loop fusion | flops 1507328 | bytes 139824 | tf_op jit(solution)/shard_map/convert_element_type | solution.py:367
  44.8 0.7 copy-done.4
  45.5 8.4 %stencils.1 = (bf16[2,768,2048]{2,1,0:T(8,128)(2,1)S(1)}, bf16[2,64,2048]{2,1,0:T(8,128)(2,1)S(1)}) custom-call(s32[2]{0:T(128)S(1)} %pad_add_fusion.where_ref, f32[12,2048]{1,0:T(8,128)S(1)} %concatenate.3.mine_ref, f32[12,2048]{1,0:T(8,128)S(1)} %collective-permute-done.1.other_ref, bf16[2,64,64]{2,1,0:T(8,128)(2,1)S(1)} %copy-done.4), custom_call_target="tpu_custom_call" | custom-call | flops 100000000 | bytes 8388608 | tf_op jit(solution)/shard_map/stencils/pallas_call | solution.py:226
  54.0 2.7 %copy-done = bf16[2,768,2048]{2,1,0:T(8,128)(2,1)} copy-done((bf16[2,768,2048]{2,1,0:T(8,128)(2,1)}, bf16[2,768,2048]{2,1,0:T(8,128)(2,1)S(1)}, u32[]{:S(2)}) %copy-start) | copy-done | bytes 6291480
  56.7 0.8 copy-done.2
  57.5 14.4 %all-to-all-done.lines_ref = bf16[64,16,1536]{2,1,0:T(8,128)(2,1)S(1)} async-done(((bf16[64,16,1536]{2,1,0:T(8,128)(2,1)}), bf16[64,16,1536]{2,1,0:T(8,128)(2,1)S(1)}, u32[]{:S(2)}, u32[]{:S(2)}) %all-to-all-start) | async-done | bytes 3145760 | tf_op jit(solution)/shard_map/all_to_all | solution.py:377
  72.0 1.0 copy-done.3
  73.0 5.1 %observe.1.part_ref = f32[2,2048]{1,0:T(2,128)S(1)} custom-call(bf16[64,1024]{1,0:T(8,128)(2,1)S(1)} %select_convert_fusion.1.rows_ref, bf16[64,16,1536]{2,1,0:T(8,128)(2,1)S(1)} %all-to-all-done.lines_ref, bf16[2,768,2048]{2,1,0:T(8,128)(2,1)} %copy-done, bf16[2,64,2048]{2,1,0:T(8,128)(2,1)S(1)} %copy-done.3), custom_call_target="tpu_custom_call" | custom-call | flops 1000000000 | bytes 10485760 | tf_op jit(solution)/shard_map/observe/pallas_call | solution.py:264
  78.1 0.1 collective-permute-start.2
  78.2 3.5 %select_convert_fusion.rows_ref = bf16[1024,64]{1,0:T(8,128)(2,1)S(1)} fusion(f32[]{:T(128)} %bitcast, f32[]{:T(128)S(6)} %sqrt.19, f32[]{:T(128)S(6)} %mul.156, f32[]{:T(128)} %bitcast.10, f32[]{:T(128)S(6)} %sqrt.18, f32[]{:T(128)S(6)} %mul.151, f32[]{:T(128)} %bitcast.8, f32[]{:T(128)S(6)} %sqrt.17, f32[]{:T(128)S(6)} %mul.146, f32[]{:T(128)} %bitcast.6, ...), kind=kLoop, calls=%fused_computation.1 | loop fusion | flops 1507328 | bytes 139824 | tf_op jit(solution)/shard_map/convert_element_type | solution.py:367
  81.7 6.3 %spread.1 = (f32[1,2048]{1,0:T(1,128)}, bf16[64,16,1536]{2,1,0:T(8,128)(2,1)S(1)}) custom-call(f32[2,2048]{1,0:T(2,128)S(1)} %observe.1.part_ref, f32[2,2048]{1,0:T(2,128)S(1)} %collective-permute-done.2.peer_ref, f32[12,2048]{1,0:T(8,128)S(1)} %concatenate.3.mine_ref, f32[12,2048]{1,0:T(8,128)S(1)} %collective-permute-done.1.other_ref, ...), custom_call_target="tpu_custom_call" | custom-call | flops 1000000000 | bytes 10485760 | tf_op jit(solution)/shard_map/spread/pallas_call | solution.py:306
  88.0 48.9 %all_to_all.10.lines_ref = bf16[64,16,1536]{2,1,0:T(8,128)(2,1)S(1)} all-to-all(bf16[64,16,1536]{2,1,0:T(8,128)(2,1)S(1)} %get-tuple-element.13), channel_id=1, replica_groups=mesh['lat'=64,'obs'=2] {'lat'}, dimensions={0} | all-to-all | bytes 6291456 | tf_op jit(solution)/shard_map/all_to_all | solution.py:381
  136.9 13.2 %backward_zonal.1 = f32[2,32,8,3072]{3,2,1,0:T(8,128)} custom-call(bf16[256,3584]{1,0:T(8,128)(2,1)S(1)} %copy-done.8, bf16[64,16,1536]{2,1,0:T(8,128)(2,1)S(1)} %all_to_all.10.lines_ref), custom_call_target="tpu_custom_call" | custom-call | flops 9663676416 | bytes 12582912 | tf_op jit(solution)/shard_map/backward_zonal/pallas_call | solution.py:174
  (42 shorter events, 0.2 us)
Async XLA Ops:
  0.6 0.7 copy-start.5
  1.3 0.7 copy-start.6
  15.8 1.6 %copy-start.1 = (bf16[64,16,1536]{2,1,0:T(8,128)(2,1)}, bf16[64,16,1536]{2,1,0:T(8,128)(2,1)S(1)}, u32[]{:S(2)}) copy-start(bf16[64,16,1536]{2,1,0:T(8,128)(2,1)S(1)} %get-tuple-element.8) | copy-start | bytes 9437188
  17.4 1.3 copy-start.7
  18.7 11.7 %copy-start.17 = (s32[1,1,2,2]{3,2,1,0:T(2,128)S(1)}, s32[1,1,2,2]{3,2,1,0:T(2,128)}, u32[]{:S(2)}) copy-start(s32[1,1,2,2]{3,2,1,0:T(2,128)} %param.19) | copy-start | bytes 52
  18.7 11.8 %copy-start.15 = (s32[1,1,2048]{2,1,0:T(1,128)S(1)}, s32[1,1,2048]{2,1,0:T(1,128)}, u32[]{:S(2)}) copy-start(s32[1,1,2048]{2,1,0:T(1,128)} %param.21) | copy-start | bytes 24580
  18.7 11.8 %copy-start.16 = (s32[1,1,2048]{2,1,0:T(1,128)S(1)}, s32[1,1,2048]{2,1,0:T(1,128)}, u32[]{:S(2)}) copy-start(s32[1,1,2048]{2,1,0:T(1,128)} %param.20) | copy-start | bytes 24580
  18.7 11.9 %copy-start.10 = (s32[1,1,4,2048]{3,2,1,0:T(4,128)S(1)}, s32[1,1,4,2048]{3,2,1,0:T(4,128)}, u32[]{:S(2)}) copy-start(s32[1,1,4,2048]{3,2,1,0:T(4,128)} %param.22) | copy-start | bytes 98308
  18.7 11.9 %copy-start.9 = (f32[1,1,4,2048]{3,2,1,0:T(4,128)S(1)}, f32[1,1,4,2048]{3,2,1,0:T(4,128)}, u32[]{:S(2)}) copy-start(f32[1,1,4,2048]{3,2,1,0:T(4,128)} %param.23) | copy-start | bytes 98308
  18.7 11.9 %copy-start.11 = (f32[1,1,2048]{2,1,0:T(1,128)S(1)}, f32[1,1,2048]{2,1,0:T(1,128)}, u32[]{:S(2)}) copy-start(f32[1,1,2048]{2,1,0:T(1,128)} %param.24) | copy-start | bytes 24580
  18.7 11.9 %copy-start.12 = (f32[1,1,2048]{2,1,0:T(1,128)S(1)}, f32[1,1,2048]{2,1,0:T(1,128)}, u32[]{:S(2)}) copy-start(f32[1,1,2048]{2,1,0:T(1,128)} %param.25) | copy-start | bytes 24580
  18.7 12.7 %copy-start.13 = (f32[4]{0:T(128)S(1)}, f32[4]{0:T(128)}, u32[]{:S(2)}) copy-start(f32[4]{0:T(128)} %param.16) | copy-start | bytes 52
  18.8 21.6 %copy-start.14 = (f32[4]{0:T(128)S(1)}, f32[4]{0:T(128)}, u32[]{:S(2)}) copy-start(f32[4]{0:T(128)} %param.17) | copy-start | bytes 52
  18.8 53.2 %all-to-all-start = ((bf16[64,16,1536]{2,1,0:T(8,128)(2,1)}), bf16[64,16,1536]{2,1,0:T(8,128)(2,1)S(1)}, u32[]{:S(2)}, u32[]{:S(2)}) async-start(bf16[64,16,1536]{2,1,0:T(8,128)(2,1)} %copy-done.1), calls=%async_computation | async-start | bytes 6291456 | tf_op jit(solution)/shard_map/all_to_all | solution.py:377
  30.4 10.5 %collective-permute-start = (s32[2,2]{1,0:T(2,128)S(1)}, s32[2,2]{1,0:T(2,128)S(1)}, u32[]{:S(2)}, u32[]{:S(2)}) collective-permute-start(s32[2,2]{1,0:T(2,128)S(1)} %bitcast.29), channel_id=1, source_target_pairs={{0,1},{1,0},{2,3},{3,2},{4,5},{5,4},{6,7},{7,6},{8,9},{9,8},{10,11... | collective-permute-start | bytes 56 | tf_op jit(solution)/shard_map/ppermute | solution.py:353
  30.8 13.9 %collective-permute-start.1 = (f32[12,2048]{1,0:T(8,128)S(1)}, f32[12,2048]{1,0:T(8,128)S(1)}, u32[]{:S(2)}, u32[]{:S(2)}) collective-permute-start(f32[12,2048]{1,0:T(8,128)S(1)} %concatenate.3.mine_ref), channel_id=1, source_target_pairs={{0,1},{1,0},{2,3},{3,2},{4,5},{5,4},{6,7},{7,6},{8,9},{9,8},{10,11... | collective-permute-start | bytes 294920 | tf_op jit(solution)/shard_map/ppermute | solution.py:351
  44.8 0.8 copy-start.4
  54.0 2.7 %copy-start = (bf16[2,768,2048]{2,1,0:T(8,128)(2,1)}, bf16[2,768,2048]{2,1,0:T(8,128)(2,1)S(1)}, u32[]{:S(2)}) copy-start(bf16[2,768,2048]{2,1,0:T(8,128)(2,1)S(1)} %get-tuple-element.9.stencil_ref) | copy-start | bytes 18874372
  56.7 0.8 copy-start.2
  72.0 1.0 copy-start.3
  73.0 5.2 %copy-start.18 = (s32[64]{0:T(128)S(1)}, s32[64]{0:T(128)}, u32[]{:S(2)}) copy-start(s32[64]{0:T(128)} %and_select_fusion) | copy-start | bytes 772
  78.1 3.6 %collective-permute-start.2 = (f32[2,2048]{1,0:T(2,128)S(1)}, f32[2,2048]{1,0:T(2,128)S(1)}, u32[]{:S(2)}, u32[]{:S(2)}) collective-permute-start(f32[2,2048]{1,0:T(2,128)S(1)} %observe.1.part_ref), channel_id=1, source_target_pairs={{0,1},{1,0},{2,3},{3,2},{4,5},{5,4},{6,7},{7,6},{8,9},{9,8},{10,11... | collective-permute-start | bytes 49160 | tf_op jit(solution)/shard_map/ppermute | solution.py:379
  88.0 48.9 %copy-start.8 = (bf16[256,3584]{1,0:T(8,128)(2,1)S(1)}, bf16[256,3584]{1,0:T(8,128)(2,1)}, u32[]{:S(2)}) copy-start(bf16[256,3584]{1,0:T(8,128)(2,1)} %copy-done.7) | copy-start | bytes 5505028

commit v2 on v1

v2 whole, which is shorter than its diff:
```python
import math

import jax
import jax.numpy as jnp
from jax import lax
from jax.experimental import pallas as pl
from jax.experimental.pallas import tpu as pltpu
from jax.sharding import PartitionSpec as P

NV = 2
LH = 32
NX = 3072
NY = 512
XW = 48
BAND = 8
NLAT = 64
GROUP = 8 * XW
LANES = LH * XW
TILE = 256
HALF = NX // 2
WIDE = 3 * TILE
EDGE = HALF - TILE
SLAB = EDGE + HALF
STEPS = HALF // WIDE
NARROW = 2 * TILE
ROWS = 16
COLS = ROWS * XW
REPORTS = 2048
SLOTS = 2
BR = 4
MIB = 2**20
LINES = NV * LH
VALUES = LINES + NV * ROWS
TABLE = VALUES + 16
FORWARD_MIB = 60
BACKWARD_MIB = 30
PREPARE_MIB = 16
OBSERVE_MIB = 45
SPREAD_MIB = 16

PIECES = (
    ((0, 48), (1, 96), (2, 128)),
    ((2, 16), (3, 64), (4, 112), (5, 128)),
    ((5, 32), (6, 80), (7, 128)),
)


def gaussians(distance, scales, heights):
    total = jnp.zeros(distance.shape, jnp.float32)
    for member in range(4):
        scale = scales[member]
        total = total + heights[member] * jnp.exp(
            -distance * distance / (2.0 * scale * scale)
        ) / jnp.sqrt(math.sqrt(math.pi) * scale)
    return total


def fill_slabs(scales_ref, heights_ref, slab_ref):
    shape = (8, NX)
    turn = lax.broadcasted_iota(jnp.int32, shape, 1) - HALF - lax.broadcasted_iota(
        jnp.int32, shape, 0
    )
    offset = jnp.abs(turn)
    distance = jnp.minimum(offset, NX - offset).astype(jnp.float32)
    scales = [scales_ref[0:1, m : m + 1] for m in range(4)]
    heights = [heights_ref[0:1, m : m + 1] for m in range(4)]
    near = gaussians(distance, scales, heights).astype(jnp.bfloat16).astype(jnp.float32)
    far = jnp.concatenate([near[:, HALF:], near[:, :HALF]], axis=1)
    for part, base in enumerate((0.5 * (near + far), 0.5 * (near - far))):
        for pair in range(TILE // 16):
            upper = base if pair == 0 else pltpu.roll(base, 16 * pair, 1)
            lower = pltpu.roll(base, 16 * pair + 8, 1)
            both = jnp.concatenate([upper, lower], axis=0)[:, TILE:]
            slab_ref[part, 16 * pair : 16 * pair + 16, :] = both.astype(jnp.bfloat16)


def zonal_columns(slab_ref, part, low, width):
    blocks = []
    for block in range(HALF // TILE):
        start = EDGE + low - TILE * block
        blocks.append(slab_ref[part, :, start : start + width])
    return jnp.concatenate(blocks, axis=0)


def zonal_halves(parts_ref, slab_ref, low, width):
    even, odd = [
        jnp.dot(
            parts_ref[part],
            zonal_columns(slab_ref, part, low, width),
            preferred_element_type=jnp.float32,
        )
        for part in range(2)
    ]
    return even + odd, even - odd


def pick(tiles, shift, lane):
    result = []
    for tile, pieces in enumerate(PIECES):
        low = 128 * tile
        value = tiles[(pieces[-1][0] - shift) % 8][:, low : low + 128]
        for block, end in pieces[-2::-1]:
            value = jnp.where(lane < end, tiles[(block - shift) % 8][:, low : low + 128], value)
        result.append(value)
    return jnp.concatenate(result, axis=1)


def forward_zonal_kernel(
    scales_hbm, heights_hbm, field_hbm, out_hbm,
    scales_ref, heights_ref, slab_ref, held_ref, parts_ref, acc_ref, out_ref, load_sems, store_sems,
):
    quarter = NV * LH * BAND // 4
    chunks = [pl.ds(quarter * k, quarter) for k in range(4)]
    loads = [
        pltpu.make_async_copy(source, target, load_sems.at[k])
        for k, (source, target) in enumerate(
            [(scales_hbm, scales_ref), (heights_hbm, heights_ref)]
            + [(field_hbm.at[chunk], held_ref.at[chunk]) for chunk in chunks]
        )
    ]
    for load in loads:
        load.start()
    loads[0].wait()
    loads[1].wait()
    fill_slabs(scales_ref, heights_ref, slab_ref)
    for k, chunk in enumerate(chunks):
        loads[2 + k].wait()
        west, east = held_ref[chunk, :HALF], held_ref[chunk, HALF:]
        parts_ref[0, chunk] = west + east
        parts_ref[1, chunk] = west - east
    lane = lax.broadcasted_iota(jnp.int32, (16, 128), 1)
    stores = []
    for step in range(STEPS):
        for side, value in enumerate(zonal_halves(parts_ref, slab_ref, WIDE * step, WIDE)):
            acc_ref[step, side] = value
        for side in range(2):
            for strips in range(2):
                first = side * (NLAT // 2) + step * 16 + strips * 8
                for group in range(LH // 8):
                    turned = []
                    for j in range(8):
                        row = (group * 8 + j) * BAND
                        both = jnp.concatenate(
                            [
                                acc_ref[step, side, v * LH * BAND + row : v * LH * BAND + row + BAND,
                                        strips * GROUP : (strips + 1) * GROUP]
                                for v in range(NV)
                            ],
                            axis=0,
                        )
                        turned.append(both if j == 0 else pltpu.roll(both, XW * j, 1))
                    for i in range(8):
                        out_ref[first + i, :, group * GROUP : (group + 1) * GROUP] = pick(
                            turned, i, lane
                        ).astype(jnp.bfloat16)
                store = pltpu.make_async_copy(
                    out_ref.at[first : first + 8], out_hbm.at[first : first + 8], store_sems.at[first // 8]
                )
                store.start()
                stores.append(store)
    for store in stores:
        store.wait()


def forward_zonal(field, scales, heights):
    rows = NV * LH * BAND
    hbm = pl.BlockSpec(memory_space=pltpu.HBM)
    return pl.pallas_call(
        forward_zonal_kernel,
        in_specs=[hbm] * 3,
        out_specs=hbm,
        out_shape=jax.ShapeDtypeStruct((NLAT, 16, LANES), jnp.bfloat16),
        scratch_shapes=[
            pltpu.VMEM((1, 4), jnp.float32),
            pltpu.VMEM((1, 4), jnp.float32),
            pltpu.VMEM((2, TILE, SLAB), jnp.bfloat16),
            pltpu.VMEM((rows, NX), jnp.bfloat16),
            pltpu.VMEM((2, rows, HALF), jnp.bfloat16),
            pltpu.VMEM((STEPS, 2, rows, WIDE), jnp.float32),
            pltpu.VMEM((NLAT, 16, LANES), jnp.bfloat16),
            pltpu.SemaphoreType.DMA((6,)),
            pltpu.SemaphoreType.DMA((NLAT // 8,)),
        ],
        compiler_params=pltpu.CompilerParams(vmem_limit_bytes=FORWARD_MIB * MIB),
        cost_estimate=pl.CostEstimate(
            flops=rows * NX * NX, bytes_accessed=8 * MIB, transcendentals=10**5
        ),
        name="forward_zonal",
    )(scales.reshape(1, 4), heights.reshape(1, 4), field)


def backward_zonal_kernel(
    slab_hbm, lines_ref, out_hbm, slab_ref, parts_ref, acc_ref, load_sem, sems
):
    load = pltpu.make_async_copy(slab_hbm, slab_ref, load_sem)
    load.start()
    lane = lax.broadcasted_iota(jnp.int32, (16, 128), 1)

    def levels(strips, group):
        tiles = [
            lines_ref[strips * 8 + i, :, group * GROUP : (group + 1) * GROUP].astype(jnp.float32)
            for i in range(8)
        ]
        picked = [pick(tiles, j, lane) for j in range(8)]
        return [p if j == 0 else pltpu.roll(p, GROUP - XW * j, 1) for j, p in enumerate(picked)]

    def fill(strips, carry):
        start = pl.multiple_of(strips * GROUP, 128)
        for group in range(LH // 8):
            west = levels(strips, group)
            east = levels(strips + NLAT // 16, group)
            for j in range(8):
                row = (group * 8 + j) * 16
                for part, value in enumerate((west[j] + east[j], west[j] - east[j])):
                    parts_ref[part, row : row + 16, pl.ds(start, GROUP)] = value.astype(
                        jnp.bfloat16
                    )
        return carry

    lax.fori_loop(0, NLAT // 16, fill, 0)
    load.wait()
    stores = []
    for step in range(HALF // NARROW):
        for side, value in enumerate(zonal_halves(parts_ref, slab_ref, NARROW * step, NARROW)):
            for level in range(LH):
                for v in range(NV):
                    row = (level * NV + v) * BAND
                    acc_ref[step, side, v, level] = value[row : row + BAND]
        for side in range(2):
            low = side * HALF + step * NARROW
            store = pltpu.make_async_copy(
                acc_ref.at[step, side], out_hbm.at[:, :, :, low : low + NARROW], sems.at[step, side]
            )
            store.start()
            stores.append(store)
    for store in stores:
        store.wait()


def backward_zonal(slab, lines):
    rows = NV * LH * BAND
    hbm = pl.BlockSpec(memory_space=pltpu.HBM)
    return pl.pallas_call(
        backward_zonal_kernel,
        in_specs=[hbm, pl.BlockSpec(memory_space=pltpu.VMEM)],
        out_specs=hbm,
        out_shape=jax.ShapeDtypeStruct((NV, LH, BAND, NX), jnp.float32),
        scratch_shapes=[
            pltpu.VMEM((2, TILE, SLAB), jnp.bfloat16),
            pltpu.VMEM((2, rows, HALF), jnp.bfloat16),
            pltpu.VMEM((HALF // NARROW, 2, NV, LH, BAND, NARROW), jnp.float32),
            pltpu.SemaphoreType.DMA,
            pltpu.SemaphoreType.DMA((HALF // NARROW, 2)),
        ],
        compiler_params=pltpu.CompilerParams(vmem_limit_bytes=BACKWARD_MIB * MIB),
        cost_estimate=pl.CostEstimate(
            flops=rows * NX * NX, bytes_accessed=12 * MIB, transcendentals=0
        ),
        name="backward_zonal",
    )(slab, lines)


def fill_stencil(table_ref, owner, stencil_ref):
    chunk = 256
    for low in range(0, REPORTS, chunk):
        part = slice(low, low + chunk)
        values = table_ref[owner, VALUES:TABLE, part].astype(jnp.float32)
        corner = values[1:2].astype(jnp.int32)
        first = values[0:1].astype(jnp.int32) * BR + corner // XW
        cell = lax.rem(corner, XW)
        column = lax.broadcasted_iota(jnp.int32, (XW, chunk), 0)
        west, east = column == cell, column == cell + 1
        lower, upper = [
            jnp.where(west, values[c : c + 1], jnp.where(east, values[c + 1 : c + 2], 0.0))
            for c in (2, 4)
        ]
        for row in range(ROWS):
            value = jnp.where(first == row, lower, jnp.where(first == row - 1, upper, 0.0))
            stencil_ref[owner, row * XW : (row + 1) * XW, part] = value.astype(jnp.bfloat16)


def prepare_kernel(
    where_ref, sends_ref, peer_sends_ref, zonal_scales_ref, zonal_heights_ref, scales_ref, heights_ref,
    mine_ref, other_ref, map_ref, table_ref, spread_ref, slab_ref,
):
    fill_slabs(zonal_scales_ref, zonal_heights_ref, slab_ref)
    strip_turn, half = where_ref[0], where_ref[1]
    shape = (LH, 2 * LH)
    slot = lax.broadcasted_iota(jnp.int32, shape, 0)
    level = (slot // 8) * 8 + lax.rem(lax.rem(slot, 8) + (8 - strip_turn), 8) + LH * half
    order = (lax.broadcasted_iota(jnp.int32, shape, 1) == level).astype(jnp.bfloat16)
    row = lax.broadcasted_iota(jnp.int32, (64, 128), 0)
    place = lax.rem(row, 4)
    for owner in range(2):
        target = half if owner == 0 else 1 - half
        for source in range(2):
            for turn in range(SLOTS):
                block = jnp.where(
                    half == source, sends_ref[target, turn], peer_sends_ref[target, turn]
                )
                chosen = (row // 32 == owner) & (
                    lax.rem(row // 4, 4) == source * SLOTS + turn
                )
                place = place + jnp.where(chosen, source * (NY // 2) + block * 4, 0)
    line = lax.broadcasted_iota(jnp.int32, (64, NLAT * 16), 1)
    apart = jnp.abs(place[:, :1] - ((line // 16) * BAND + lax.rem(line, BAND))).astype(jnp.float32)
    matrix = gaussians(
        apart,
        [scales_ref[0:1, m : m + 1] for m in range(4)],
        [heights_ref[0:1, m : m + 1] for m in range(4)],
    )
    own = lax.rem(row // ROWS, NV)[:, :1] == lax.rem(line // BAND, NV)
    matrix = jnp.where(own, matrix, 0.0)
    spread_ref[...] = matrix.T.astype(jnp.bfloat16)
    matrix = matrix.astype(jnp.bfloat16)
    blank = jnp.zeros((NV * ROWS, REPORTS - NLAT * 16), jnp.bfloat16)
    for owner in range(2):
        table_ref[owner, LINES:VALUES, : NLAT * 16] = matrix[owner * 32 : (owner + 1) * 32]
        table_ref[owner, LINES:VALUES, NLAT * 16 :] = blank
    for owner, ref in enumerate((mine_ref, other_ref)):
        code = ref[1:2, :].astype(jnp.int32)
        for v in range(NV):
            rows = lax.broadcasted_iota(jnp.int32, (2 * LH, REPORTS), 0) + 2 * LH * v
            hot = (rows == code).astype(jnp.float32).astype(jnp.bfloat16)
            picked = lax.dot_general(
                map_ref[v], hot, (((0,), (0,)), ((), ())), preferred_element_type=jnp.float32
            ).astype(jnp.bfloat16)
            table_ref[owner, v * LH : (v + 1) * LH, :] = jnp.dot(
                order, picked, preferred_element_type=jnp.float32
            ).astype(jnp.bfloat16)
        values = [ref[0:1, :], ref[2:3, :], ref[6:10, :]]
        for row in (10, 11):
            rest = ref[row : row + 1, :]
            for _ in range(3):
                term = rest.astype(jnp.bfloat16).astype(jnp.float32)
                values.append(term)
                rest = rest - term
        values.append(jnp.zeros((4, REPORTS), jnp.float32))
        table_ref[owner, VALUES:TABLE, :] = jnp.concatenate(values, axis=0).astype(jnp.bfloat16)


def prepare(where, sends, peer_sends, zonal, meridional, mine, other, vertical_map):
    smem = pl.BlockSpec(memory_space=pltpu.SMEM)
    vmem = pl.BlockSpec(memory_space=pltpu.VMEM)
    return pl.pallas_call(
        prepare_kernel,
        in_specs=[smem] * 3 + [vmem] * 7,
        out_shape=[
            jax.ShapeDtypeStruct((2, TABLE, REPORTS), jnp.bfloat16),
            jax.ShapeDtypeStruct((NLAT * 16, 64), jnp.bfloat16),
            jax.ShapeDtypeStruct((2, TILE, SLAB), jnp.bfloat16),
        ],
        compiler_params=pltpu.CompilerParams(vmem_limit_bytes=PREPARE_MIB * MIB),
        cost_estimate=pl.CostEstimate(
            flops=10**9, bytes_accessed=8 * MIB, transcendentals=3 * 10**5
        ),
        name="prepare",
    )(where, sends, peer_sends, *[x.reshape(1, 4) for x in zonal + meridional], mine, other, vertical_map)


def observe_kernel(
    table_hbm, rows_hbm, lines_ref, out_ref, stencil_ref, table_ref, rows_ref, pick_ref, grid_ref, sems
):
    loads = [
        pltpu.make_async_copy(table_hbm, table_ref, sems.at[0]),
        pltpu.make_async_copy(rows_hbm, rows_ref, sems.at[1]),
    ]
    for load in loads:
        load.start()
    loads[0].wait()
    rows = jnp.concatenate([table_ref[o, LINES:VALUES, : NLAT * 16] for o in range(2)], axis=0)
    lines = lines_ref[...].reshape(NLAT * 16, LANES)
    mixed = jnp.dot(rows, lines, preferred_element_type=jnp.float32)
    mixed = mixed.astype(jnp.bfloat16).astype(jnp.float32)
    for level in range(LH):
        pick_ref[level * 64 : (level + 1) * 64, :XW] = mixed[:, level * XW : (level + 1) * XW]
    for owner in range(2):
        for v in range(NV):
            for row in range(ROWS):
                start = (owner * NV + v) * ROWS + row
                column = owner * COLS + row * XW
                grid_ref[v * LH : (v + 1) * LH, column : column + XW] = pick_ref[
                    pl.ds(start, LH, stride=64), :
                ][:, :XW]
    for owner in range(2):
        fill_stencil(table_ref, owner, stencil_ref)
        points = grid_ref[:, owner * COLS : (owner + 1) * COLS].astype(jnp.bfloat16)
        columns = jnp.dot(points, stencil_ref[owner], preferred_element_type=jnp.float32)
        out_ref[owner : owner + 1, :] = jnp.sum(
            columns * table_ref[owner, :LINES, :].astype(jnp.float32), axis=0, keepdims=True
        )
    loads[1].wait()


def observe(table, rows, lines):
    hbm = pl.BlockSpec(memory_space=pltpu.HBM)
    vmem = pl.BlockSpec(memory_space=pltpu.VMEM)
    return pl.pallas_call(
        observe_kernel,
        in_specs=[hbm, hbm, vmem],
        out_specs=[vmem] * 4,
        out_shape=[
            pltpu.VMEM((2, REPORTS), jnp.float32),
            pltpu.VMEM((2, COLS, REPORTS), jnp.bfloat16),
            pltpu.VMEM(table.shape, jnp.bfloat16),
            pltpu.VMEM(rows.shape, jnp.bfloat16),
        ],
        scratch_shapes=[
            pltpu.VMEM((LH * 64, 128), jnp.float32),
            pltpu.VMEM((NV * LH, 2 * COLS), jnp.float32),
            pltpu.SemaphoreType.DMA((2,)),
        ],
        compiler_params=pltpu.CompilerParams(vmem_limit_bytes=OBSERVE_MIB * MIB),
        cost_estimate=pl.CostEstimate(
            flops=10**9, bytes_accessed=10 * MIB, transcendentals=0
        ),
        name="observe",
    )(table, rows, lines)


def spread_kernel(part_ref, peer_ref, stencil_ref, table_ref, rows_ref, departure_ref, out_ref, pick_ref):
    for owner in range(2):
        value = part_ref[owner : owner + 1, :] + peer_ref[1 - owner : 2 - owner, :]
        terms = table_ref[owner, VALUES:TABLE, :].astype(jnp.float32)
        innovation, precision = [
            terms[k : k + 1] + terms[k + 1 : k + 2] + terms[k + 2 : k + 3] for k in (6, 9)
        ]
        departure = precision * (value - innovation)
        if owner == 0:
            departure_ref[...] = departure
        level = table_ref[owner, :LINES, :].astype(jnp.float32)
        pushed = (level * departure).astype(jnp.bfloat16)
        lifted = lax.dot_general(
            pushed,
            stencil_ref[owner],
            (((1,), (1,)), ((), ())),
            preferred_element_type=jnp.float32,
        )
        lifted = jnp.concatenate([lifted, jnp.zeros((NV * LH, 128), jnp.float32)], axis=1)
        for v in range(NV):
            for row in range(ROWS):
                start = (owner * NV + v) * ROWS + row
                pick_ref[pl.ds(start, LH, stride=64), :] = lifted[
                    v * LH : (v + 1) * LH, row * XW : row * XW + 128
                ]
    parts = [pick_ref[level * 64 : (level + 1) * 64, :][:, :XW] for level in range(LH)]
    lines = jnp.concatenate(parts, axis=1).astype(jnp.bfloat16)
    out = jnp.dot(rows_ref[...], lines, preferred_element_type=jnp.float32)
    out_ref[...] = out.astype(jnp.bfloat16).reshape(NLAT, 16, LANES)


def spread(part, peer, held):
    vmem = pl.BlockSpec(memory_space=pltpu.VMEM)
    return pl.pallas_call(
        spread_kernel,
        in_specs=[vmem] * 5,
        out_shape=[
            jax.ShapeDtypeStruct((1, REPORTS), jnp.float32),
            jax.ShapeDtypeStruct((NLAT, 16, LANES), jnp.bfloat16),
        ],
        scratch_shapes=[pltpu.VMEM((LH * 64, 128), jnp.float32)],
        compiler_params=pltpu.CompilerParams(vmem_limit_bytes=SPREAD_MIB * MIB),
        cost_estimate=pl.CostEstimate(
            flops=10**9, bytes_accessed=10 * MIB, transcendentals=0
        ),
        name="spread",
    )(part, peer, *held)


def on_device(
    control,
    zonal_scales,
    zonal_heights,
    meridional_scales,
    meridional_heights,
    vertical_map,
    send_blocks,
    report_slot,
    report_level,
    report_corner,
    report_weight,
    innovation,
    report_precision,
):
    strip = lax.axis_index("lat")
    half = lax.axis_index("obs")
    swap = [(0, 1), (1, 0)]

    mine = jnp.concatenate(
        [
            report_slot.reshape(1, -1).astype(jnp.float32),
            report_level.reshape(1, -1).astype(jnp.float32),
            report_corner.reshape(4, -1).astype(jnp.float32),
            report_weight.reshape(4, -1),
            innovation.reshape(1, -1),
            report_precision.reshape(1, -1),
        ],
        axis=0,
    )
    other = lax.ppermute(mine, "obs", swap)
    sends = send_blocks.reshape(2, 2)
    peer_sends = lax.ppermute(sends, "obs", swap)
    where = jnp.stack([strip % 8, half]).astype(jnp.int32)
    table, spread_rows, slab = prepare(
        where,
        sends,
        peer_sends,
        (zonal_scales, zonal_heights),
        (meridional_scales, meridional_heights),
        mine,
        other,
        vertical_map,
    )

    smoothed = forward_zonal(control.reshape(NV * LH * BAND, NX), zonal_scales, zonal_heights)
    lines = lax.all_to_all(smoothed, "lat", split_axis=0, concat_axis=0, tiled=True)
    part, *held = observe(table, spread_rows, lines)
    peer = lax.ppermute(part, "obs", swap)
    departure, back = spread(part, peer, held)
    back = lax.all_to_all(back, "lat", split_axis=0, concat_axis=0, tiled=True)
    gradient = backward_zonal(slab, back)
    return departure.reshape(report_slot.shape), gradient


def solution(mesh):
    in_specs = (
        P(None, "obs", "lat", None),
        P(),
        P(),
        P(),
        P(),
        P(),
        P("lat", "obs", None, None),
        P("lat", "obs", None),
        P("lat", "obs", None),
        P("lat", "obs", None, None),
        P("lat", "obs", None, None),
        P("lat", "obs", None),
        P("lat", "obs", None),
    )
    out_specs = (P("lat", "obs", None), P(None, "obs", "lat", None))
    return jax.shard_map(
        on_device, mesh=mesh, in_specs=in_specs, out_specs=out_specs, check_vma=False
    )
```

time: 151 us -> 131 us (0.87)
  waiting for transfers between devices: 14.4 us -> 37.5 us
  Pallas kernels: 46.8 us -> 29 us
  local copies, waits for them, and re-layouts: 11.4 us -> 1.9 us
  other arithmetic: 7.66 us -> 0.1 us
  between operations: 8.51 us -> 1.03 us
    all_to_all x1, waiting for transfers between devices: 14.4 us -> 35.5 us  [on_device(): lax.all_to_all(smoothed, 'lat', split_axis=0, concat_axis=0, tiled=True)]
    pallas_call x5, Pallas kernels: 46.8 us -> 29 us  [the longest x1 9.04 us: forward_zonal(): pl.pallas_call(forward_zonal_kernel, in_specs=[hbm] * 3, out_specs=hbm, o...]
    unnamed x38 -> x28, local copies, waits for them, and re-layouts: 9.57 us -> 1.67 us
    convert_element_type x2 -> x0, other arithmetic: 6.96 us -> none  [meridional(): return jnp.where(av == bv, matrix, 0.0).astype(jnp.bfloat16)]
  transfers between devices with their start and end apart: 4 -> 4, of which waited for: 1 -> 3; matrix products, arithmetic and copies ran while one was open for 6% -> 0% of each run, Pallas kernels for 6% -> 2%
where the time goes in v2:
time: 131 us
  blocking collectives  48.7 us (37%)
  waiting for transfers between devices  37.5 us (29%)
  Pallas kernels  29 us (22%)
  starting transfers between devices  12.8 us (10%)
  local copies, waits for them, and re-layouts  1.9 us (1%)
    all_to_all x1, blocking collectives, on_device(): back = lax.all_to_all(back, 'lat', split_axis=0, concat_axis=0, tiled=True)  48.7 us
    all_to_all x1, waiting for transfers between devices, on_device(): lax.all_to_all(smoothed, 'lat', split_axis=0, concat_axis=0, tiled=True)  35.5 us
    all_to_all x1, starting transfers between devices, on_device(): lax.all_to_all(smoothed, 'lat', split_axis=0, concat_axis=0, tiled=True)  11.9 us
    pallas_call x1, Pallas kernels, forward_zonal(): pl.pallas_call(forward_zonal_kernel, in_specs=[hbm] * 3, out_specs=hbm, o...  9.04 us
    pallas_call x1, Pallas kernels, backward_zonal(): pl.pallas_call(backward_zonal_kernel, in_specs=[hbm, pl.BlockSpec(memory_...  8.14 us
    pallas_call x1, Pallas kernels, observe(): pl.pallas_call(observe_kernel, in_specs=[hbm, hbm, vmem], out_specs=[vmem...  5.68 us
    pallas_call x1, Pallas kernels, spread(): pl.pallas_call(spread_kernel, in_specs=[vmem] * 5, out_shape=[jax.ShapeDt...  3.99 us
  transfers between devices with their start and end apart: 4, of which 3 were waited for; matrix products, arithmetic and copies ran while one was open for 0% of the time, Pallas kernels for 2%

profile of v2, /device:TPU:0, one launch (start us, length us, event | category | flops | bytes accessed | tf_op | source)
XLA Modules:
  0.0 131.1 jit_solution(7724333680129942967)
XLA Ops:
  0.6 9.0 %forward_zonal.1 = bf16[64,16,1536]{2,1,0:T(8,128)(2,1)} custom-call(f32[1,4]{1,0:T(1,128)} %bitcast.20, f32[1,4]{1,0:T(1,128)} %bitcast.22, bf16[512,3072]{1,0:T(8,128)(2,1)} %bitcast.29), custom_call_target="tpu_custom_call" | custom-call | flops 4831838208 | bytes 8388608 | tf_op jit(solution)/shard_map/forward_zonal/pallas_call | solution.py:168
  9.7 0.0 copy-start.1
  9.7 0.0 copy-start.12
  9.7 0.0 copy-start.13
  9.7 0.0 copy-start.9
  9.7 0.0 copy-start.8
  9.7 0.0 copy-start.10
  9.7 0.0 copy-start.11
  9.8 0.0 copy-start
  9.8 0.0 copy-start.2
  9.8 0.0 copy-start.3
  9.8 0.0 copy-start.4
  9.8 0.0 copy-start.5
  9.8 11.9 %all-to-all-start = ((bf16[64,16,1536]{2,1,0:T(8,128)(2,1)}), bf16[64,16,1536]{2,1,0:T(8,128)(2,1)}, u32[]{:S(2)}, u32[]{:S(2)}) async-start(bf16[64,16,1536]{2,1,0:T(8,128)(2,1)} %forward_zonal.1), calls=%async_computation | async-start | bytes 6291456 | tf_op jit(solution)/shard_map/all_to_all | solution.py:516
  21.7 0.1 collective-permute-start
  21.9 0.0 copy-done.8
  21.9 0.0 copy-done.10
  21.9 0.0 copy-done.11
  21.9 0.2 concatenate.3.mine_ref
  22.1 0.7 collective-permute-start.1
  22.9 0.1 pad_add_fusion.where_ref
  22.9 0.0 collective-permute-done.peer_sends_ref
  22.9 0.9 collective-permute-done.1.other_ref
  23.9 2.2 %prepare.1 = (bf16[2,112,2048]{2,1,0:T(8,128)(2,1)S(1)}, bf16[1024,64]{1,0:T(8,128)(2,1)S(1)}, bf16[2,256,2816]{2,1,0:T(8,128)(2,1)S(1)}) custom-call(s32[2]{0:T(128)S(1)} %pad_add_fusion.where_ref, s32[2,2]{1,0:T(2,128)S(1)} %bitcast.19, s32[2,2]{1,0:T(2,128)S(1)} %collective-permute-done.peer_sends_ref, f32[1,4]{1,0:T(1,128)S(1)} %bitcast.21, ...), custom_call_target="tpu_custom_call" | custom-call | flops 1000000000 | bytes 8388608 | tf_op jit(solution)/shard_map/prepare/pallas_call | solution.py:345
  26.1 1.6 %copy-done.6 = bf16[2,256,2816]{2,1,0:T(8,128)(2,1)} copy-done((bf16[2,256,2816]{2,1,0:T(8,128)(2,1)}, bf16[2,256,2816]{2,1,0:T(8,128)(2,1)S(1)}, u32[]{:S(2)}) %copy-start.6) | copy-done | bytes 2883608
  27.6 35.5 %all-to-all-done.lines_ref = bf16[64,16,1536]{2,1,0:T(8,128)(2,1)} async-done(((bf16[64,16,1536]{2,1,0:T(8,128)(2,1)}), bf16[64,16,1536]{2,1,0:T(8,128)(2,1)}, u32[]{:S(2)}, u32[]{:S(2)}) %all-to-all-start) | async-done | bytes 3145760 | tf_op jit(solution)/shard_map/all_to_all | solution.py:516
  63.1 5.7 %observe.1 = (f32[2,2048]{1,0:T(2,128)S(1)}, bf16[2,768,2048]{2,1,0:T(8,128)(2,1)S(1)}, bf16[2,112,2048]{2,1,0:T(8,128)(2,1)S(1)}, bf16[1024,64]{1,0:T(8,128)(2,1)S(1)}) custom-call(bf16[2,112,2048]{2,1,0:T(8,128)(2,1)S(1)} %get-tuple-element.11.table_hbm, bf16[1024,64]{1,0:T(8,128)(2,1)S(1)} %get-tuple-element.12.rows_hbm, ...), custom_call_target="tpu_custom_call" | custom-call | flops 1000000000 | bytes 10485760 | tf_op jit(solution)/shard_map/observe/pallas_call | solution.py:398
  68.8 0.1 collective-permute-start.2
  68.9 1.2 collective-permute-done.2.peer_ref
  70.1 4.0 %spread.1 = (f32[1,2048]{1,0:T(1,128)}, bf16[64,16,1536]{2,1,0:T(8,128)(2,1)S(1)}) custom-call(f32[2,2048]{1,0:T(2,128)S(1)} %get-tuple-element.13.part_ref, f32[2,2048]{1,0:T(2,128)S(1)} %collective-permute-done.2.peer_ref, bf16[2,768,2048]{2,1,0:T(8,128)(2,1)S(1)} %get-tuple-element.14.stencil_ref, bf16[2,112,2048]{2,1,0:T(8,128)(2,1)S(1)} %get-tuple-element.15.table_ref, ...), custom_call_target="tpu_custom_call" | custom-call | flops 1000000000 | bytes 10485760 | tf_op jit(solution)/shard_map/spread/pallas_call | solution.py:454
  74.1 48.7 %all_to_all.10.lines_ref = bf16[64,16,1536]{2,1,0:T(8,128)(2,1)S(1)} all-to-all(bf16[64,16,1536]{2,1,0:T(8,128)(2,1)S(1)} %get-tuple-element.19), channel_id=1, replica_groups=mesh['lat'=64,'obs'=2] {'lat'}, dimensions={0} | all-to-all | bytes 6291456 | tf_op jit(solution)/shard_map/all_to_all | solution.py:520
  122.8 8.1 %backward_zonal.1 = f32[2,32,8,3072]{3,2,1,0:T(8,128)} custom-call(bf16[2,256,2816]{2,1,0:T(8,128)(2,1)S(1)} %copy-done.7, bf16[64,16,1536]{2,1,0:T(8,128)(2,1)S(1)} %all_to_all.10.lines_ref), custom_call_target="tpu_custom_call" | custom-call | flops 4831838208 | bytes 12582912 | tf_op jit(solution)/shard_map/backward_zonal/pallas_call | solution.py:243
  (14 shorter events, 0.0 us)
Async XLA Ops:
  9.7 12.0 %copy-start.1 = (s32[1,1,2,2]{3,2,1,0:T(2,128)S(1)}, s32[1,1,2,2]{3,2,1,0:T(2,128)}, u32[]{:S(2)}) copy-start(s32[1,1,2,2]{3,2,1,0:T(2,128)} %param.19) | copy-start | bytes 52
  9.7 12.1 %copy-start.12 = (s32[1,1,2048]{2,1,0:T(1,128)S(1)}, s32[1,1,2048]{2,1,0:T(1,128)}, u32[]{:S(2)}) copy-start(s32[1,1,2048]{2,1,0:T(1,128)} %param.21) | copy-start | bytes 24580
  9.7 12.1 %copy-start.13 = (s32[1,1,2048]{2,1,0:T(1,128)S(1)}, s32[1,1,2048]{2,1,0:T(1,128)}, u32[]{:S(2)}) copy-start(s32[1,1,2048]{2,1,0:T(1,128)} %param.20) | copy-start | bytes 24580
  9.7 12.1 %copy-start.9 = (s32[1,1,4,2048]{3,2,1,0:T(4,128)S(1)}, s32[1,1,4,2048]{3,2,1,0:T(4,128)}, u32[]{:S(2)}) copy-start(s32[1,1,4,2048]{3,2,1,0:T(4,128)} %param.22) | copy-start | bytes 98308
  9.7 12.1 %copy-start.8 = (f32[1,1,4,2048]{3,2,1,0:T(4,128)S(1)}, f32[1,1,4,2048]{3,2,1,0:T(4,128)}, u32[]{:S(2)}) copy-start(f32[1,1,4,2048]{3,2,1,0:T(4,128)} %param.23) | copy-start | bytes 98308
  9.7 12.1 %copy-start.10 = (f32[1,1,2048]{2,1,0:T(1,128)S(1)}, f32[1,1,2048]{2,1,0:T(1,128)}, u32[]{:S(2)}) copy-start(f32[1,1,2048]{2,1,0:T(1,128)} %param.24) | copy-start | bytes 24580
  9.7 12.1 %copy-start.11 = (f32[1,1,2048]{2,1,0:T(1,128)S(1)}, f32[1,1,2048]{2,1,0:T(1,128)}, u32[]{:S(2)}) copy-start(f32[1,1,2048]{2,1,0:T(1,128)} %param.25) | copy-start | bytes 24580
  9.8 14.1 %copy-start = (bf16[2,64,64]{2,1,0:T(8,128)(2,1)S(1)}, bf16[2,64,64]{2,1,0:T(8,128)(2,1)}, u32[]{:S(2)}) copy-start(bf16[2,64,64]{2,1,0:T(8,128)(2,1)} %map_ref.1) | copy-start | bytes 49156
  9.8 14.1 %copy-start.2 = (f32[4]{0:T(128)S(1)}, f32[4]{0:T(128)}, u32[]{:S(2)}) copy-start(f32[4]{0:T(128)} %param.14) | copy-start | bytes 52
  9.8 14.1 %copy-start.3 = (f32[4]{0:T(128)S(1)}, f32[4]{0:T(128)}, u32[]{:S(2)}) copy-start(f32[4]{0:T(128)} %param.15) | copy-start | bytes 52
  9.8 14.1 %copy-start.4 = (f32[4]{0:T(128)S(1)}, f32[4]{0:T(128)}, u32[]{:S(2)}) copy-start(f32[4]{0:T(128)} %param.16) | copy-start | bytes 52
  9.8 14.1 %copy-start.5 = (f32[4]{0:T(128)S(1)}, f32[4]{0:T(128)}, u32[]{:S(2)}) copy-start(f32[4]{0:T(128)} %param.17) | copy-start | bytes 52
  9.8 53.3 %all-to-all-start = ((bf16[64,16,1536]{2,1,0:T(8,128)(2,1)}), bf16[64,16,1536]{2,1,0:T(8,128)(2,1)}, u32[]{:S(2)}, u32[]{:S(2)}) async-start(bf16[64,16,1536]{2,1,0:T(8,128)(2,1)} %forward_zonal.1), calls=%async_computation | async-start | bytes 6291456 | tf_op jit(solution)/shard_map/all_to_all | solution.py:516
  21.7 1.2 collective-permute-start
  22.1 1.7 %collective-permute-start.1 = (f32[12,2048]{1,0:T(8,128)S(1)}, f32[12,2048]{1,0:T(8,128)S(1)}, u32[]{:S(2)}, u32[]{:S(2)}) collective-permute-start(f32[12,2048]{1,0:T(8,128)S(1)} %concatenate.3.mine_ref), channel_id=1, source_target_pairs={{0,1},{1,0},{2,3},{3,2},{4,5},{5,4},{6,7},{7,6},{8,9},{9,8},{10,11... | collective-permute-start | bytes 294920 | tf_op jit(solution)/shard_map/ppermute | solution.py:500
  26.1 1.6 %copy-start.6 = (bf16[2,256,2816]{2,1,0:T(8,128)(2,1)}, bf16[2,256,2816]{2,1,0:T(8,128)(2,1)S(1)}, u32[]{:S(2)}) copy-start(bf16[2,256,2816]{2,1,0:T(8,128)(2,1)S(1)} %get-tuple-element.18.slab_hbm) | copy-start | bytes 8650756
  68.8 1.3 collective-permute-start.2
  74.1 48.7 %copy-start.7 = (bf16[2,256,2816]{2,1,0:T(8,128)(2,1)S(1)}, bf16[2,256,2816]{2,1,0:T(8,128)(2,1)}, u32[]{:S(2)}) copy-start(bf16[2,256,2816]{2,1,0:T(8,128)(2,1)} %copy-done.6) | copy-start | bytes 8650756

commit v3 on v2

--- a/solution.py
+++ b/solution.py
@@ -18,11 +18,10 @@
 LANES = LH * XW
 TILE = 256
 HALF = NX // 2
-WIDE = 3 * TILE
-EDGE = HALF - TILE
-SLAB = EDGE + HALF
-STEPS = HALF // WIDE
-NARROW = 2 * TILE
+QUARTER = NX // 4
+SLAB_SUM = 2 * HALF - TILE
+SLAB_DIFFERENCE = SLAB_SUM + 2 * QUARTER - TILE
+SLAB = SLAB_DIFFERENCE + 2 * QUARTER - TILE
 ROWS = 16
 COLS = ROWS * XW
 REPORTS = 2048
@@ -66,32 +65,48 @@
     heights = [heights_ref[0:1, m : m + 1] for m in range(4)]
     near = gaussians(distance, scales, heights).astype(jnp.bfloat16).astype(jnp.float32)
     far = jnp.concatenate([near[:, HALF:], near[:, :HALF]], axis=1)
-    for part, base in enumerate((0.5 * (near + far), 0.5 * (near - far))):
+    total = near + far
+    shifted = jnp.concatenate([total[:, QUARTER:], total[:, :QUARTER]], axis=1)
+    for base, low, high, length in (
+        (0.5 * (near - far), 0, SLAB_SUM, HALF),
+        (0.25 * (total + shifted), SLAB_SUM, SLAB_DIFFERENCE, QUARTER),
+        (0.25 * (total - shifted), SLAB_DIFFERENCE, SLAB, QUARTER),
+    ):
+        first = HALF - length + TILE
         for pair in range(TILE // 16):
             upper = base if pair == 0 else pltpu.roll(base, 16 * pair, 1)
             lower = pltpu.roll(base, 16 * pair + 8, 1)
-            both = jnp.concatenate([upper, lower], axis=0)[:, TILE:]
-            slab_ref[part, 16 * pair : 16 * pair + 16, :] = both.astype(jnp.bfloat16)
-
-
-def zonal_columns(slab_ref, part, low, width):
+            both = jnp.concatenate([upper, lower], axis=0)[:, first : first + high - low]
+            slab_ref[16 * pair : 16 * pair + 16, low:high] = both.astype(jnp.bfloat16)
+
+
+def zonal_part(parts_ref, slab_ref, first, start, length, low, width):
     blocks = []
-    for block in range(HALF // TILE):
-        start = EDGE + low - TILE * block
-        blocks.append(slab_ref[part, :, start : start + width])
-    return jnp.concatenate(blocks, axis=0)
-
-
-def zonal_halves(parts_ref, slab_ref, low, width):
-    even, odd = [
-        jnp.dot(
-            parts_ref[part],
-            zonal_columns(slab_ref, part, low, width),
-            preferred_element_type=jnp.float32,
-        )
-        for part in range(2)
-    ]
-    return even + odd, even - odd
+    for block in range(length // TILE):
+        left = start + length - TILE + low - TILE * block
+        blocks.append(slab_ref[:, left : left + width])
+    return jnp.dot(
+        parts_ref[:, first : first + length],
+        jnp.concatenate(blocks, axis=0),
+        preferred_element_type=jnp.float32,
+    )
+
+
+def zonal_quarters(parts_ref, slab_ref, low, width):
+    total = zonal_part(parts_ref, slab_ref, HALF, SLAB_SUM, QUARTER, low, width)
+    change = zonal_part(
+        parts_ref, slab_ref, HALF + QUARTER, SLAB_DIFFERENCE, QUARTER, low, width
+    )
+    west = zonal_part(parts_ref, slab_ref, 0, 0, HALF, low, width)
+    east = zonal_part(parts_ref, slab_ref, 0, 0, HALF, QUARTER + low, width)
+    first, second = total + change, total - change
+    return first + west, second + east, first - west, second - east
+
+
+def zonal_split(quarters):
+    first, second = quarters[0] + quarters[2], quarters[1] + quarters[3]
+    pieces = (quarters[0] - quarters[2], quarters[1] - quarters[3], first + second, first - second)
+    return [piece.astype(jnp.bfloat16) for piece in pieces]
 
 
 def pick(tiles, shift, lane):
@@ -125,39 +140,41 @@
     fill_slabs(scales_ref, heights_ref, slab_ref)
     for k, chunk in enumerate(chunks):
         loads[2 + k].wait()
-        west, east = held_ref[chunk, :HALF], held_ref[chunk, HALF:]
-        parts_ref[0, chunk] = west + east
-        parts_ref[1, chunk] = west - east
+        quarters = [
+            held_ref[chunk, QUARTER * q : QUARTER * (q + 1)].astype(jnp.float32) for q in range(4)
+        ]
+        for q, piece in enumerate(zonal_split(quarters)):
+            parts_ref[chunk, QUARTER * q : QUARTER * (q + 1)] = piece
     lane = lax.broadcasted_iota(jnp.int32, (16, 128), 1)
     stores = []
-    for step in range(STEPS):
-        for side, value in enumerate(zonal_halves(parts_ref, slab_ref, WIDE * step, WIDE)):
-            acc_ref[step, side] = value
-        for side in range(2):
-            for strips in range(2):
-                first = side * (NLAT // 2) + step * 16 + strips * 8
-                for group in range(LH // 8):
-                    turned = []
-                    for j in range(8):
-                        row = (group * 8 + j) * BAND
-                        both = jnp.concatenate(
-                            [
-                                acc_ref[step, side, v * LH * BAND + row : v * LH * BAND + row + BAND,
-                                        strips * GROUP : (strips + 1) * GROUP]
-                                for v in range(NV)
-                            ],
-                            axis=0,
-                        )
-                        turned.append(both if j == 0 else pltpu.roll(both, XW * j, 1))
-                    for i in range(8):
-                        out_ref[first + i, :, group * GROUP : (group + 1) * GROUP] = pick(
-                            turned, i, lane
-                        ).astype(jnp.bfloat16)
-                store = pltpu.make_async_copy(
-                    out_ref.at[first : first + 8], out_hbm.at[first : first + 8], store_sems.at[first // 8]
-                )
-                store.start()
-                stores.append(store)
+    for q, value in enumerate(zonal_quarters(parts_ref, slab_ref, 0, QUARTER)):
+        acc_ref[q] = value
+    for q in range(4):
+        for strips in range(2):
+            first = q * 16 + strips * 8
+            for group in range(LH // 8):
+                turned = []
+                for j in range(8):
+                    row = (group * 8 + j) * BAND
+                    both = jnp.concatenate(
+                        [
+                            acc_ref[q, v * LH * BAND + row : v * LH * BAND + row + BAND,
+                                    strips * GROUP : (strips + 1) * GROUP]
+                            for v in range(NV)
+                        ],
+                        axis=0,
+                    )
+                    both = both if j == 0 else pltpu.roll(both, XW * j, 1)
+                    turned.append(both.astype(jnp.bfloat16))
+                for i in range(8):
+                    out_ref[first + i, :, group * GROUP : (group + 1) * GROUP] = pick(
+                        turned, i, lane
+                    )
+            store = pltpu.make_async_copy(
+                out_ref.at[first : first + 8], out_hbm.at[first : first + 8], store_sems.at[first // 8]
+            )
+            store.start()
+            stores.append(store)
     for store in stores:
         store.wait()
 
@@ -173,10 +190,10 @@
         scratch_shapes=[
             pltpu.VMEM((1, 4), jnp.float32),
             pltpu.VMEM((1, 4), jnp.float32),
-            pltpu.VMEM((2, TILE, SLAB), jnp.bfloat16),
+            pltpu.VMEM((TILE, SLAB), jnp.bfloat16),
             pltpu.VMEM((rows, NX), jnp.bfloat16),
-            pltpu.VMEM((2, rows, HALF), jnp.bfloat16),
-            pltpu.VMEM((STEPS, 2, rows, WIDE), jnp.float32),
+            pltpu.VMEM((rows, NX), jnp.bfloat16),
+            pltpu.VMEM((4, rows, QUARTER), jnp.float32),
             pltpu.VMEM((NLAT, 16, LANES), jnp.bfloat16),
             pltpu.SemaphoreType.DMA((6,)),
             pltpu.SemaphoreType.DMA((NLAT // 8,)),
@@ -198,38 +215,35 @@
 
     def levels(strips, group):
         tiles = [
-            lines_ref[strips * 8 + i, :, group * GROUP : (group + 1) * GROUP].astype(jnp.float32)
-            for i in range(8)
+            lines_ref[strips * 8 + i, :, group * GROUP : (group + 1) * GROUP] for i in range(8)
         ]
-        picked = [pick(tiles, j, lane) for j in range(8)]
+        picked = [pick(tiles, j, lane).astype(jnp.float32) for j in range(8)]
         return [p if j == 0 else pltpu.roll(p, GROUP - XW * j, 1) for j, p in enumerate(picked)]
 
     def fill(strips, carry):
-        start = pl.multiple_of(strips * GROUP, 128)
         for group in range(LH // 8):
-            west = levels(strips, group)
-            east = levels(strips + NLAT // 16, group)
+            quarters = [levels(strips + NLAT // 32 * q, group) for q in range(4)]
             for j in range(8):
                 row = (group * 8 + j) * 16
-                for part, value in enumerate((west[j] + east[j], west[j] - east[j])):
-                    parts_ref[part, row : row + 16, pl.ds(start, GROUP)] = value.astype(
-                        jnp.bfloat16
-                    )
+                for q, piece in enumerate(zonal_split([quarter[j] for quarter in quarters])):
+                    start = pl.multiple_of(strips * GROUP + q * QUARTER, 128)
+                    parts_ref[row : row + 16, pl.ds(start, GROUP)] = piece
         return carry
 
-    lax.fori_loop(0, NLAT // 16, fill, 0)
+    lax.fori_loop(0, NLAT // 32, fill, 0)
     load.wait()
     stores = []
-    for step in range(HALF // NARROW):
-        for side, value in enumerate(zonal_halves(parts_ref, slab_ref, NARROW * step, NARROW)):
+    for step in range(QUARTER // TILE):
+        low = step * TILE
+        for q, value in enumerate(zonal_quarters(parts_ref, slab_ref, low, TILE)):
             for level in range(LH):
                 for v in range(NV):
                     row = (level * NV + v) * BAND
-                    acc_ref[step, side, v, level] = value[row : row + BAND]
-        for side in range(2):
-            low = side * HALF + step * NARROW
+                    acc_ref[step, q, v, level] = value[row : row + BAND]
+        for q in range(4):
+            left = q * QUARTER + low
             store = pltpu.make_async_copy(
-                acc_ref.at[step, side], out_hbm.at[:, :, :, low : low + NARROW], sems.at[step, side]
+                acc_ref.at[step, q], out_hbm.at[:, :, :, left : left + TILE], sems.at[step, q]
             )
             store.start()
             stores.append(store)
@@ -246,11 +260,11 @@
         out_specs=hbm,
         out_shape=jax.ShapeDtypeStruct((NV, LH, BAND, NX), jnp.float32),
         scratch_shapes=[
-            pltpu.VMEM((2, TILE, SLAB), jnp.bfloat16),
-            pltpu.VMEM((2, rows, HALF), jnp.bfloat16),
-            pltpu.VMEM((HALF // NARROW, 2, NV, LH, BAND, NARROW), jnp.float32),
+            pltpu.VMEM((TILE, SLAB), jnp.bfloat16),
+            pltpu.VMEM((rows, NX), jnp.bfloat16),
+            pltpu.VMEM((QUARTER // TILE, 4, NV, LH, BAND, TILE), jnp.float32),
             pltpu.SemaphoreType.DMA,
-            pltpu.SemaphoreType.DMA((HALF // NARROW, 2)),
+            pltpu.SemaphoreType.DMA((QUARTER // TILE, 4)),
         ],
         compiler_params=pltpu.CompilerParams(vmem_limit_bytes=BACKWARD_MIB * MIB),
         cost_estimate=pl.CostEstimate(
@@ -281,7 +295,7 @@
 
 def prepare_kernel(
     where_ref, sends_ref, peer_sends_ref, zonal_scales_ref, zonal_heights_ref, scales_ref, heights_ref,
-    mine_ref, other_ref, map_ref, table_ref, spread_ref, slab_ref,
+    mine_ref, other_ref, map_ref, table_ref, spread_ref, slab_ref, turned_ref, column_ref,
 ):
     fill_slabs(zonal_scales_ref, zonal_heights_ref, slab_ref)
     strip_turn, half = where_ref[0], where_ref[1]
@@ -336,7 +350,22 @@
                 values.append(term)
                 rest = rest - term
         values.append(jnp.zeros((4, REPORTS), jnp.float32))
-        table_ref[owner, VALUES:TABLE, :] = jnp.concatenate(values, axis=0).astype(jnp.bfloat16)
+        values = jnp.concatenate(values, axis=0)
+        table_ref[owner, VALUES:TABLE, :] = values.astype(jnp.bfloat16)
+        column_ref[...] = values.T
+
+        def turn_stencil(step, carry):
+            start = pl.multiple_of(step * 128, 128)
+            columns = column_ref[pl.ds(start, 128), :]
+            point = (columns[:, 0:1] * float(BR * XW) + columns[:, 1:2]).astype(jnp.int32)
+            apart = lax.broadcasted_iota(jnp.int32, (128, COLS), 1) - point
+            value = jnp.zeros((128, COLS), jnp.float32)
+            for c, offset in enumerate((0, 1, XW, XW + 1)):
+                value = jnp.where(apart == offset, columns[:, 2 + c : 3 + c], value)
+            turned_ref[owner, pl.ds(start, 128), :] = value.astype(jnp.bfloat16)
+            return carry
+
+        lax.fori_loop(0, REPORTS // 128, turn_stencil, 0)
 
 
 def prepare(where, sends, peer_sends, zonal, meridional, mine, other, vertical_map):
@@ -348,8 +377,10 @@
         out_shape=[
             jax.ShapeDtypeStruct((2, TABLE, REPORTS), jnp.bfloat16),
             jax.ShapeDtypeStruct((NLAT * 16, 64), jnp.bfloat16),
-            jax.ShapeDtypeStruct((2, TILE, SLAB), jnp.bfloat16),
-        ],
+            jax.ShapeDtypeStruct((TILE, SLAB), jnp.bfloat16),
+            jax.ShapeDtypeStruct((2, REPORTS, COLS), jnp.bfloat16),
+        ],
+        scratch_shapes=[pltpu.VMEM((REPORTS, 16), jnp.float32)],
         compiler_params=pltpu.CompilerParams(vmem_limit_bytes=PREPARE_MIB * MIB),
         cost_estimate=pl.CostEstimate(
             flops=10**9, bytes_accessed=8 * MIB, transcendentals=3 * 10**5
@@ -359,15 +390,18 @@
 
 
 def observe_kernel(
-    table_hbm, rows_hbm, lines_ref, out_ref, stencil_ref, table_ref, rows_ref, pick_ref, grid_ref, sems
+    table_hbm, rows_hbm, turned_hbm, lines_ref, out_ref, table_ref, rows_ref, turned_ref,
+    stencil_ref, pick_ref, grid_ref, sems,
 ):
     loads = [
         pltpu.make_async_copy(table_hbm, table_ref, sems.at[0]),
         pltpu.make_async_copy(rows_hbm, rows_ref, sems.at[1]),
+        pltpu.make_async_copy(turned_hbm, turned_ref, sems.at[2]),
     ]
-    for load in loads:
-        load.start()
+    loads[0].start()
     loads[0].wait()
+    loads[1].start()
+    loads[2].start()
     rows = jnp.concatenate([table_ref[o, LINES:VALUES, : NLAT * 16] for o in range(2)], axis=0)
     lines = lines_ref[...].reshape(NLAT * 16, LANES)
     mixed = jnp.dot(rows, lines, preferred_element_type=jnp.float32)
@@ -390,35 +424,37 @@
             columns * table_ref[owner, :LINES, :].astype(jnp.float32), axis=0, keepdims=True
         )
     loads[1].wait()
-
-
-def observe(table, rows, lines):
+    loads[2].wait()
+
+
+def observe(table, rows, turned, lines):
     hbm = pl.BlockSpec(memory_space=pltpu.HBM)
     vmem = pl.BlockSpec(memory_space=pltpu.VMEM)
     return pl.pallas_call(
         observe_kernel,
-        in_specs=[hbm, hbm, vmem],
+        in_specs=[hbm, hbm, hbm, vmem],
         out_specs=[vmem] * 4,
         out_shape=[
             pltpu.VMEM((2, REPORTS), jnp.float32),
-            pltpu.VMEM((2, COLS, REPORTS), jnp.bfloat16),
             pltpu.VMEM(table.shape, jnp.bfloat16),
             pltpu.VMEM(rows.shape, jnp.bfloat16),
+            pltpu.VMEM(turned.shape, jnp.bfloat16),
         ],
         scratch_shapes=[
+            pltpu.VMEM((2, COLS, REPORTS), jnp.bfloat16),
             pltpu.VMEM((LH * 64, 128), jnp.float32),
             pltpu.VMEM((NV * LH, 2 * COLS), jnp.float32),
-            pltpu.SemaphoreType.DMA((2,)),
+            pltpu.SemaphoreType.DMA((3,)),
         ],
         compiler_params=pltpu.CompilerParams(vmem_limit_bytes=OBSERVE_MIB * MIB),
         cost_estimate=pl.CostEstimate(
             flops=10**9, bytes_accessed=10 * MIB, transcendentals=0
         ),
         name="observe",
-    )(table, rows, lines)
-
-
-def spread_kernel(part_ref, peer_ref, stencil_ref, table_ref, rows_ref, departure_ref, out_ref, pick_ref):
+    )(table, rows, turned, lines)
+
+
+def spread_kernel(part_ref, peer_ref, table_ref, rows_ref, turned_ref, departure_ref, out_ref, pick_ref):
     for owner in range(2):
         value = part_ref[owner : owner + 1, :] + peer_ref[1 - owner : 2 - owner, :]
         terms = table_ref[owner, VALUES:TABLE, :].astype(jnp.float32)
@@ -430,12 +466,7 @@
             departure_ref[...] = departure
         level = table_ref[owner, :LINES, :].astype(jnp.float32)
         pushed = (level * departure).astype(jnp.bfloat16)
-        lifted = lax.dot_general(
-            pushed,
-            stencil_ref[owner],
-            (((1,), (1,)), ((), ())),
-            preferred_element_type=jnp.float32,
-        )
+        lifted = jnp.dot(pushed, turned_ref[owner], preferred_element_type=jnp.float32)
         lifted = jnp.concatenate([lifted, jnp.zeros((NV * LH, 128), jnp.float32)], axis=1)
         for v in range(NV):
             for row in range(ROWS):
@@ -501,7 +532,7 @@
     sends = send_blocks.reshape(2, 2)
     peer_sends = lax.ppermute(sends, "obs", swap)
     where = jnp.stack([strip % 8, half]).astype(jnp.int32)
-    table, spread_rows, slab = prepare(
+    table, spread_rows, slab, turned = prepare(
         where,
         sends,
         peer_sends,
@@ -514,7 +545,8 @@
 
     smoothed = forward_zonal(control.reshape(NV * LH * BAND, NX), zonal_scales, zonal_heights)
     lines = lax.all_to_all(smoothed, "lat", split_axis=0, concat_axis=0, tiled=True)
-    part, *held = observe(table, spread_rows, lines)
+    lines = pltpu.with_memory_space_constraint(lines, pltpu.VMEM)
+    part, *held = observe(table, spread_rows, turned, lines)
     peer = lax.ppermute(part, "obs", swap)
     departure, back = spread(part, peer, held)
     back = lax.all_to_all(back, "lat", split_axis=0, concat_axis=0, tiled=True)

time: 131 us -> 127 us (0.969)
  waiting for transfers between devices: 37.5 us -> 24.2 us
  Pallas kernels: 29 us -> 34.3 us
  local copies, waits for them, and re-layouts: 1.9 us -> 6.21 us
    all_to_all x1, waiting for transfers between devices: 35.5 us -> 22.1 us  [on_device(): lax.all_to_all(smoothed, 'lat', split_axis=0, concat_axis=0, tiled=True)]
    pallas_call x1, Pallas kernels: 2.17 us -> 11.4 us  [prepare(): pl.pallas_call(prepare_kernel, in_specs=[smem] * 3 + [vmem] * 7, out_shap...]
    unnamed x28 -> x34, local copies, waits for them, and re-layouts: 1.67 us -> 5.98 us
  transfers between devices with their start and end apart: 4 -> 4, of which waited for: 3 -> 3; matrix products, arithmetic and copies ran while one was open for 0% -> 0% of each run, Pallas kernels for 2% -> 9%
where the time goes in v3:
time: 127 us
  blocking collectives  48.7 us (38%)
  Pallas kernels  34.3 us (27%)
  waiting for transfers between devices  24.2 us (19%)
  starting transfers between devices  12.5 us (10%)
  local copies, waits for them, and re-layouts  6.21 us (5%)
    all_to_all x1, blocking collectives, on_device(): back = lax.all_to_all(back, 'lat', split_axis=0, concat_axis=0, tiled=True)  48.7 us
    all_to_all x1, waiting for transfers between devices, on_device(): lax.all_to_all(smoothed, 'lat', split_axis=0, concat_axis=0, tiled=True)  22.1 us
    all_to_all x1, starting transfers between devices, on_device(): lax.all_to_all(smoothed, 'lat', split_axis=0, concat_axis=0, tiled=True)  11.6 us
    pallas_call x1, Pallas kernels, prepare(): pl.pallas_call(prepare_kernel, in_specs=[smem] * 3 + [vmem] * 7, out_shap...  11.4 us
    pallas_call x1, Pallas kernels, forward_zonal(): pl.pallas_call(forward_zonal_kernel, in_specs=[hbm] * 3, out_specs=hbm, o...  7.83 us
    pallas_call x1, Pallas kernels, backward_zonal(): pl.pallas_call(backward_zonal_kernel, in_specs=[hbm, pl.BlockSpec(memory_...  7.39 us
    unnamed x34, local copies, waits for them, and re-layouts  5.98 us
    pallas_call x1, Pallas kernels, observe(): pl.pallas_call(observe_kernel, in_specs=[hbm, hbm, hbm, vmem], out_specs=...  4.51 us
  transfers between devices with their start and end apart: 4, of which 3 were waited for; matrix products, arithmetic and copies ran while one was open for 0% of the time, Pallas kernels for 9%

profile of v3, /device:TPU:0, one launch (start us, length us, event | category | flops | bytes accessed | tf_op | source)
XLA Modules:
  0.0 127.1 jit_solution(252974908890299498)
XLA Ops:
  0.6 7.8 %forward_zonal.1 = bf16[64,16,1536]{2,1,0:T(8,128)(2,1)} custom-call(f32[1,4]{1,0:T(1,128)} %bitcast.20, f32[1,4]{1,0:T(1,128)} %bitcast.22, bf16[512,3072]{1,0:T(8,128)(2,1)} %bitcast.29), custom_call_target="tpu_custom_call" | custom-call | flops 4831838208 | bytes 8388608 | tf_op jit(solution)/shard_map/forward_zonal/pallas_call | solution.py:185
  8.5 0.0 copy-start.4
  8.5 0.0 copy-start.15
  8.5 0.0 copy-start.16
  8.5 0.0 copy-start.12
  8.5 0.0 copy-start.11
  8.5 0.0 copy-start.13
  8.5 0.0 copy-start.14
  8.6 0.0 copy-start.3
  8.6 0.0 copy-start.5
  8.6 0.0 copy-start.6
  8.6 0.0 copy-start.7
  8.6 0.0 copy-start.8
  8.6 11.6 %all-to-all-start = ((bf16[64,16,1536]{2,1,0:T(8,128)(2,1)}), bf16[64,16,1536]{2,1,0:T(8,128)(2,1)S(1)}, u32[]{:S(2)}, u32[]{:S(2)}) async-start(bf16[64,16,1536]{2,1,0:T(8,128)(2,1)} %forward_zonal.1), calls=%async_computation | async-start | bytes 6291456 | tf_op jit(solution)/shard_map/all_to_all | solution.py:547
  20.3 0.1 collective-permute-start
  20.5 0.2 concatenate.3.mine_ref
  20.7 0.7 collective-permute-start.1
  21.4 0.1 pad_add_fusion.where_ref
  21.5 0.9 collective-permute-done.1.other_ref
  22.4 11.4 %prepare.1 = (bf16[2,112,2048]{2,1,0:T(8,128)(2,1)S(1)}, bf16[1024,64]{1,0:T(8,128)(2,1)S(1)}, bf16[256,5376]{1,0:T(8,128)(2,1)S(1)}, bf16[2,2048,768]{2,1,0:T(8,128)(2,1)S(1)}) custom-call(s32[2]{0:T(128)S(1)} %pad_add_fusion.where_ref, s32[2,2]{1,0:T(2,128)S(1)} %bitcast.19, s32[2,2]{1,0:T(2,128)S(1)} %collective-permute-done.peer_sends_ref, ...), custom_call_target="tpu_custom_call" | custom-call | flops 1000000000 | bytes 8388608 | tf_op jit(solution)/shard_map/prepare/pallas_call | solution.py:374
  33.8 0.0 copy-start
  33.8 2.7 %copy-done = bf16[2,2048,768]{2,1,0:T(8,128)(2,1)} copy-done((bf16[2,2048,768]{2,1,0:T(8,128)(2,1)}, bf16[2,2048,768]{2,1,0:T(8,128)(2,1)S(1)}, u32[]{:S(2)}) %copy-start) | copy-done | bytes 6291480
  36.5 0.9 copy-done.1
  37.5 0.7 copy-done.2
  38.2 1.5 %copy-done.9 = bf16[256,5376]{1,0:T(8,128)(2,1)} copy-done((bf16[256,5376]{1,0:T(8,128)(2,1)}, bf16[256,5376]{1,0:T(8,128)(2,1)S(1)}, u32[]{:S(2)}) %copy-start.9) | copy-done | bytes 2752536
  39.7 22.1 %all-to-all-done.lines_ref = bf16[64,16,1536]{2,1,0:T(8,128)(2,1)S(1)} async-done(((bf16[64,16,1536]{2,1,0:T(8,128)(2,1)}), bf16[64,16,1536]{2,1,0:T(8,128)(2,1)S(1)}, u32[]{:S(2)}, u32[]{:S(2)}) %all-to-all-start) | async-done | bytes 3145760 | tf_op jit(solution)/shard_map/all_to_all | solution.py:547
  61.8 4.5 %observe.1 = (f32[2,2048]{1,0:T(2,128)S(1)}, bf16[2,112,2048]{2,1,0:T(8,128)(2,1)S(1)}, bf16[1024,64]{1,0:T(8,128)(2,1)S(1)}, bf16[2,2048,768]{2,1,0:T(8,128)(2,1)S(1)}) custom-call(bf16[2,112,2048]{2,1,0:T(8,128)(2,1)} %copy-done.1, bf16[1024,64]{1,0:T(8,128)(2,1)} %copy-done.2, bf16[2,2048,768]{2,1,0:T(8,128)(2,1)} %copy-done, ...), custom_call_target="tpu_custom_call" | custom-call | flops 1000000000 | bytes 10485760 | tf_op jit(solution)/shard_map/observe/pallas_call | solution.py:433
  66.3 0.1 collective-permute-start.2
  66.4 1.2 collective-permute-done.2.peer_ref
  67.6 3.2 %spread.1 = (f32[1,2048]{1,0:T(1,128)}, bf16[64,16,1536]{2,1,0:T(8,128)(2,1)S(1)}) custom-call(f32[2,2048]{1,0:T(2,128)S(1)} %get-tuple-element.15.part_ref, f32[2,2048]{1,0:T(2,128)S(1)} %collective-permute-done.2.peer_ref, bf16[2,112,2048]{2,1,0:T(8,128)(2,1)S(1)} %get-tuple-element.16.table_ref, bf16[1024,64]{1,0:T(8,128)(2,1)S(1)} %get-tuple-element.17.rows_ref, ...), custom_call_target="tpu_custom_call" | custom-call | flops 1000000000 | bytes 10485760 | tf_op jit(solution)/shard_map/spread/pallas_call | solution.py:485
  70.8 48.7 %all_to_all.10.lines_ref = bf16[64,16,1536]{2,1,0:T(8,128)(2,1)S(1)} all-to-all(bf16[64,16,1536]{2,1,0:T(8,128)(2,1)S(1)} %get-tuple-element.21), channel_id=1, replica_groups=mesh['lat'=64,'obs'=2] {'lat'}, dimensions={0} | all-to-all | bytes 6291456 | tf_op jit(solution)/shard_map/all_to_all | solution.py:552
  119.5 7.4 %backward_zonal.1 = f32[2,32,8,3072]{3,2,1,0:T(8,128)} custom-call(bf16[256,5376]{1,0:T(8,128)(2,1)S(1)} %copy-done.10, bf16[64,16,1536]{2,1,0:T(8,128)(2,1)S(1)} %all_to_all.10.lines_ref), custom_call_target="tpu_custom_call" | custom-call | flops 4831838208 | bytes 12582912 | tf_op jit(solution)/shard_map/backward_zonal/pallas_call | solution.py:257
  (20 shorter events, 0.1 us)
Async XLA Ops:
  8.5 11.8 %copy-start.4 = (s32[1,1,2,2]{3,2,1,0:T(2,128)S(1)}, s32[1,1,2,2]{3,2,1,0:T(2,128)}, u32[]{:S(2)}) copy-start(s32[1,1,2,2]{3,2,1,0:T(2,128)} %param.19) | copy-start | bytes 52
  8.5 11.9 %copy-start.15 = (s32[1,1,2048]{2,1,0:T(1,128)S(1)}, s32[1,1,2048]{2,1,0:T(1,128)}, u32[]{:S(2)}) copy-start(s32[1,1,2048]{2,1,0:T(1,128)} %param.21) | copy-start | bytes 24580
  8.5 11.9 %copy-start.16 = (s32[1,1,2048]{2,1,0:T(1,128)S(1)}, s32[1,1,2048]{2,1,0:T(1,128)}, u32[]{:S(2)}) copy-start(s32[1,1,2048]{2,1,0:T(1,128)} %param.20) | copy-start | bytes 24580
  8.5 11.9 %copy-start.12 = (s32[1,1,4,2048]{3,2,1,0:T(4,128)S(1)}, s32[1,1,4,2048]{3,2,1,0:T(4,128)}, u32[]{:S(2)}) copy-start(s32[1,1,4,2048]{3,2,1,0:T(4,128)} %param.22) | copy-start | bytes 98308
  8.5 11.9 %copy-start.11 = (f32[1,1,4,2048]{3,2,1,0:T(4,128)S(1)}, f32[1,1,4,2048]{3,2,1,0:T(4,128)}, u32[]{:S(2)}) copy-start(f32[1,1,4,2048]{3,2,1,0:T(4,128)} %param.23) | copy-start | bytes 98308
  8.5 11.9 %copy-start.13 = (f32[1,1,2048]{2,1,0:T(1,128)S(1)}, f32[1,1,2048]{2,1,0:T(1,128)}, u32[]{:S(2)}) copy-start(f32[1,1,2048]{2,1,0:T(1,128)} %param.24) | copy-start | bytes 24580
  8.5 11.9 %copy-start.14 = (f32[1,1,2048]{2,1,0:T(1,128)S(1)}, f32[1,1,2048]{2,1,0:T(1,128)}, u32[]{:S(2)}) copy-start(f32[1,1,2048]{2,1,0:T(1,128)} %param.25) | copy-start | bytes 24580
  8.6 13.9 %copy-start.3 = (bf16[2,64,64]{2,1,0:T(8,128)(2,1)S(1)}, bf16[2,64,64]{2,1,0:T(8,128)(2,1)}, u32[]{:S(2)}) copy-start(bf16[2,64,64]{2,1,0:T(8,128)(2,1)} %map_ref.1) | copy-start | bytes 49156
  8.6 13.9 %copy-start.5 = (f32[4]{0:T(128)S(1)}, f32[4]{0:T(128)}, u32[]{:S(2)}) copy-start(f32[4]{0:T(128)} %param.14) | copy-start | bytes 52
  8.6 13.8 %copy-start.6 = (f32[4]{0:T(128)S(1)}, f32[4]{0:T(128)}, u32[]{:S(2)}) copy-start(f32[4]{0:T(128)} %param.15) | copy-start | bytes 52
  8.6 13.8 %copy-start.7 = (f32[4]{0:T(128)S(1)}, f32[4]{0:T(128)}, u32[]{:S(2)}) copy-start(f32[4]{0:T(128)} %param.16) | copy-start | bytes 52
  8.6 13.8 %copy-start.8 = (f32[4]{0:T(128)S(1)}, f32[4]{0:T(128)}, u32[]{:S(2)}) copy-start(f32[4]{0:T(128)} %param.17) | copy-start | bytes 52
  8.6 53.2 %all-to-all-start = ((bf16[64,16,1536]{2,1,0:T(8,128)(2,1)}), bf16[64,16,1536]{2,1,0:T(8,128)(2,1)S(1)}, u32[]{:S(2)}, u32[]{:S(2)}) async-start(bf16[64,16,1536]{2,1,0:T(8,128)(2,1)} %forward_zonal.1), calls=%async_computation | async-start | bytes 6291456 | tf_op jit(solution)/shard_map/all_to_all | solution.py:547
  20.3 1.2 collective-permute-start
  20.7 1.7 %collective-permute-start.1 = (f32[12,2048]{1,0:T(8,128)S(1)}, f32[12,2048]{1,0:T(8,128)S(1)}, u32[]{:S(2)}, u32[]{:S(2)}) collective-permute-start(f32[12,2048]{1,0:T(8,128)S(1)} %concatenate.3.mine_ref), channel_id=1, source_target_pairs={{0,1},{1,0},{2,3},{3,2},{4,5},{5,4},{6,7},{7,6},{8,9},{9,8},{10,11... | collective-permute-start | bytes 294920 | tf_op jit(solution)/shard_map/ppermute | solution.py:531
  33.8 2.7 %copy-start = (bf16[2,2048,768]{2,1,0:T(8,128)(2,1)}, bf16[2,2048,768]{2,1,0:T(8,128)(2,1)S(1)}, u32[]{:S(2)}) copy-start(bf16[2,2048,768]{2,1,0:T(8,128)(2,1)S(1)} %get-tuple-element.14.turned_hbm) | copy-start | bytes 18874372
  36.5 0.9 copy-start.1
  37.5 0.7 copy-start.2
  38.2 1.5 %copy-start.9 = (bf16[256,5376]{1,0:T(8,128)(2,1)}, bf16[256,5376]{1,0:T(8,128)(2,1)S(1)}, u32[]{:S(2)}) copy-start(bf16[256,5376]{1,0:T(8,128)(2,1)S(1)} %get-tuple-element.20.slab_hbm) | copy-start | bytes 8257540
  66.3 1.3 collective-permute-start.2
  70.8 48.7 %copy-start.10 = (bf16[256,5376]{1,0:T(8,128)(2,1)S(1)}, bf16[256,5376]{1,0:T(8,128)(2,1)}, u32[]{:S(2)}) copy-start(bf16[256,5376]{1,0:T(8,128)(2,1)} %copy-done.9) | copy-start | bytes 8257540

commit v4 on v3

--- a/solution.py
+++ b/solution.py
@@ -148,7 +148,7 @@
     lane = lax.broadcasted_iota(jnp.int32, (16, 128), 1)
     stores = []
     for q, value in enumerate(zonal_quarters(parts_ref, slab_ref, 0, QUARTER)):
-        acc_ref[q] = value
+        acc_ref[q] = value.astype(jnp.bfloat16)
     for q in range(4):
         for strips in range(2):
             first = q * 16 + strips * 8
@@ -159,7 +159,7 @@
                     both = jnp.concatenate(
                         [
                             acc_ref[q, v * LH * BAND + row : v * LH * BAND + row + BAND,
-                                    strips * GROUP : (strips + 1) * GROUP]
+                                    strips * GROUP : (strips + 1) * GROUP].astype(jnp.float32)
                             for v in range(NV)
                         ],
                         axis=0,
@@ -193,7 +193,7 @@
             pltpu.VMEM((TILE, SLAB), jnp.bfloat16),
             pltpu.VMEM((rows, NX), jnp.bfloat16),
             pltpu.VMEM((rows, NX), jnp.bfloat16),
-            pltpu.VMEM((4, rows, QUARTER), jnp.float32),
+            pltpu.VMEM((4, rows, QUARTER), jnp.bfloat16),
             pltpu.VMEM((NLAT, 16, LANES), jnp.bfloat16),
             pltpu.SemaphoreType.DMA((6,)),
             pltpu.SemaphoreType.DMA((NLAT // 8,)),
@@ -220,17 +220,17 @@
         picked = [pick(tiles, j, lane).astype(jnp.float32) for j in range(8)]
         return [p if j == 0 else pltpu.roll(p, GROUP - XW * j, 1) for j, p in enumerate(picked)]
 
-    def fill(strips, carry):
+    def fill(strips):
         for group in range(LH // 8):
             quarters = [levels(strips + NLAT // 32 * q, group) for q in range(4)]
             for j in range(8):
                 row = (group * 8 + j) * 16
                 for q, piece in enumerate(zonal_split([quarter[j] for quarter in quarters])):
-                    start = pl.multiple_of(strips * GROUP + q * QUARTER, 128)
-                    parts_ref[row : row + 16, pl.ds(start, GROUP)] = piece
-        return carry
-
-    lax.fori_loop(0, NLAT // 32, fill, 0)
+                    start = strips * GROUP + q * QUARTER
+                    parts_ref[row : row + 16, start : start + GROUP] = piece
+
+    for strips in range(NLAT // 32):
+        fill(strips)
     load.wait()
     stores = []
     for step in range(QUARTER // TILE):

time: 127 us -> 127 us (level)
  no operation moved by 1% of the time
where the time goes in v4:
time: 127 us
  blocking collectives  48.7 us (38%)
  Pallas kernels  34.2 us (27%)
  waiting for transfers between devices  24.2 us (19%)
  starting transfers between devices  12.5 us (10%)
  local copies, waits for them, and re-layouts  6.21 us (5%)
    all_to_all x1, blocking collectives, on_device(): back = lax.all_to_all(back, 'lat', split_axis=0, concat_axis=0, tiled=True)  48.7 us
    all_to_all x1, waiting for transfers between devices, on_device(): lax.all_to_all(smoothed, 'lat', split_axis=0, concat_axis=0, tiled=True)  22.1 us
    all_to_all x1, starting transfers between devices, on_device(): lax.all_to_all(smoothed, 'lat', split_axis=0, concat_axis=0, tiled=True)  11.6 us
    pallas_call x1, Pallas kernels, prepare(): pl.pallas_call(prepare_kernel, in_specs=[smem] * 3 + [vmem] * 7, out_shap...  11.4 us
    pallas_call x1, Pallas kernels, forward_zonal(): pl.pallas_call(forward_zonal_kernel, in_specs=[hbm] * 3, out_specs=hbm, o...  7.69 us
    pallas_call x1, Pallas kernels, backward_zonal(): pl.pallas_call(backward_zonal_kernel, in_specs=[hbm, pl.BlockSpec(memory_...  7.4 us
    unnamed x34, local copies, waits for them, and re-layouts  5.98 us
    pallas_call x1, Pallas kernels, observe(): pl.pallas_call(observe_kernel, in_specs=[hbm, hbm, hbm, vmem], out_specs=...  4.51 us
  transfers between devices with their start and end apart: 4, of which 3 were waited for; matrix products, arithmetic and copies ran while one was open for 0% of the time, Pallas kernels for 9%

profile of v4, /device:TPU:0, one launch (start us, length us, event | category | flops | bytes accessed | tf_op | source)
XLA Modules:
  0.0 127.0 jit_solution(4252682635407938135)
XLA Ops:
  0.6 7.7 %forward_zonal.1 = bf16[64,16,1536]{2,1,0:T(8,128)(2,1)} custom-call(f32[1,4]{1,0:T(1,128)} %bitcast.20, f32[1,4]{1,0:T(1,128)} %bitcast.22, bf16[512,3072]{1,0:T(8,128)(2,1)} %bitcast.29), custom_call_target="tpu_custom_call" | custom-call | flops 4831838208 | bytes 8388608 | tf_op jit(solution)/shard_map/forward_zonal/pallas_call | solution.py:185
  8.3 0.0 copy-start.4
  8.3 0.0 copy-start.15
  8.4 0.0 copy-start.16
  8.4 0.0 copy-start.12
  8.4 0.0 copy-start.11
  8.4 0.0 copy-start.13
  8.4 0.0 copy-start.14
  8.4 0.0 copy-start.3
  8.4 0.0 copy-start.5
  8.4 0.0 copy-start.6
  8.5 0.0 copy-start.7
  8.5 0.0 copy-start.8
  8.5 11.6 %all-to-all-start = ((bf16[64,16,1536]{2,1,0:T(8,128)(2,1)}), bf16[64,16,1536]{2,1,0:T(8,128)(2,1)S(1)}, u32[]{:S(2)}, u32[]{:S(2)}) async-start(bf16[64,16,1536]{2,1,0:T(8,128)(2,1)} %forward_zonal.1), calls=%async_computation | async-start | bytes 6291456 | tf_op jit(solution)/shard_map/all_to_all | solution.py:547
  20.1 0.1 collective-permute-start
  20.3 0.2 concatenate.3.mine_ref
  20.6 0.7 collective-permute-start.1
  21.3 0.1 pad_add_fusion.where_ref
  21.4 0.9 collective-permute-done.1.other_ref
  22.3 11.4 %prepare.1 = (bf16[2,112,2048]{2,1,0:T(8,128)(2,1)S(1)}, bf16[1024,64]{1,0:T(8,128)(2,1)S(1)}, bf16[256,5376]{1,0:T(8,128)(2,1)S(1)}, bf16[2,2048,768]{2,1,0:T(8,128)(2,1)S(1)}) custom-call(s32[2]{0:T(128)S(1)} %pad_add_fusion.where_ref, s32[2,2]{1,0:T(2,128)S(1)} %bitcast.19, s32[2,2]{1,0:T(2,128)S(1)} %collective-permute-done.peer_sends_ref, ...), custom_call_target="tpu_custom_call" | custom-call | flops 1000000000 | bytes 8388608 | tf_op jit(solution)/shard_map/prepare/pallas_call | solution.py:374
  33.7 0.0 copy-start
  33.7 2.7 %copy-done = bf16[2,2048,768]{2,1,0:T(8,128)(2,1)} copy-done((bf16[2,2048,768]{2,1,0:T(8,128)(2,1)}, bf16[2,2048,768]{2,1,0:T(8,128)(2,1)S(1)}, u32[]{:S(2)}) %copy-start) | copy-done | bytes 6291480
  36.4 0.9 copy-done.1
  37.3 0.7 copy-done.2
  38.0 1.5 %copy-done.9 = bf16[256,5376]{1,0:T(8,128)(2,1)} copy-done((bf16[256,5376]{1,0:T(8,128)(2,1)}, bf16[256,5376]{1,0:T(8,128)(2,1)S(1)}, u32[]{:S(2)}) %copy-start.9) | copy-done | bytes 2752536
  39.6 22.1 %all-to-all-done.lines_ref = bf16[64,16,1536]{2,1,0:T(8,128)(2,1)S(1)} async-done(((bf16[64,16,1536]{2,1,0:T(8,128)(2,1)}), bf16[64,16,1536]{2,1,0:T(8,128)(2,1)S(1)}, u32[]{:S(2)}, u32[]{:S(2)}) %all-to-all-start) | async-done | bytes 3145760 | tf_op jit(solution)/shard_map/all_to_all | solution.py:547
  61.7 4.5 %observe.1 = (f32[2,2048]{1,0:T(2,128)S(1)}, bf16[2,112,2048]{2,1,0:T(8,128)(2,1)S(1)}, bf16[1024,64]{1,0:T(8,128)(2,1)S(1)}, bf16[2,2048,768]{2,1,0:T(8,128)(2,1)S(1)}) custom-call(bf16[2,112,2048]{2,1,0:T(8,128)(2,1)} %copy-done.1, bf16[1024,64]{1,0:T(8,128)(2,1)} %copy-done.2, bf16[2,2048,768]{2,1,0:T(8,128)(2,1)} %copy-done, ...), custom_call_target="tpu_custom_call" | custom-call | flops 1000000000 | bytes 10485760 | tf_op jit(solution)/shard_map/observe/pallas_call | solution.py:433
  66.2 0.1 collective-permute-start.2
  66.3 1.2 collective-permute-done.2.peer_ref
  67.4 3.2 %spread.1 = (f32[1,2048]{1,0:T(1,128)}, bf16[64,16,1536]{2,1,0:T(8,128)(2,1)S(1)}) custom-call(f32[2,2048]{1,0:T(2,128)S(1)} %get-tuple-element.15.part_ref, f32[2,2048]{1,0:T(2,128)S(1)} %collective-permute-done.2.peer_ref, bf16[2,112,2048]{2,1,0:T(8,128)(2,1)S(1)} %get-tuple-element.16.table_ref, bf16[1024,64]{1,0:T(8,128)(2,1)S(1)} %get-tuple-element.17.rows_ref, ...), custom_call_target="tpu_custom_call" | custom-call | flops 1000000000 | bytes 10485760 | tf_op jit(solution)/shard_map/spread/pallas_call | solution.py:485
  70.7 48.7 %all_to_all.10.lines_ref = bf16[64,16,1536]{2,1,0:T(8,128)(2,1)S(1)} all-to-all(bf16[64,16,1536]{2,1,0:T(8,128)(2,1)S(1)} %get-tuple-element.21), channel_id=1, replica_groups=mesh['lat'=64,'obs'=2] {'lat'}, dimensions={0} | all-to-all | bytes 6291456 | tf_op jit(solution)/shard_map/all_to_all | solution.py:552
  119.4 7.4 %backward_zonal.1 = f32[2,32,8,3072]{3,2,1,0:T(8,128)} custom-call(bf16[256,5376]{1,0:T(8,128)(2,1)S(1)} %copy-done.10, bf16[64,16,1536]{2,1,0:T(8,128)(2,1)S(1)} %all_to_all.10.lines_ref), custom_call_target="tpu_custom_call" | custom-call | flops 4831838208 | bytes 12582912 | tf_op jit(solution)/shard_map/backward_zonal/pallas_call | solution.py:257
  (20 shorter events, 0.1 us)
Async XLA Ops:
  8.3 11.8 %copy-start.4 = (s32[1,1,2,2]{3,2,1,0:T(2,128)S(1)}, s32[1,1,2,2]{3,2,1,0:T(2,128)}, u32[]{:S(2)}) copy-start(s32[1,1,2,2]{3,2,1,0:T(2,128)} %param.19) | copy-start | bytes 52
  8.3 11.9 %copy-start.15 = (s32[1,1,2048]{2,1,0:T(1,128)S(1)}, s32[1,1,2048]{2,1,0:T(1,128)}, u32[]{:S(2)}) copy-start(s32[1,1,2048]{2,1,0:T(1,128)} %param.21) | copy-start | bytes 24580
  8.4 11.9 %copy-start.16 = (s32[1,1,2048]{2,1,0:T(1,128)S(1)}, s32[1,1,2048]{2,1,0:T(1,128)}, u32[]{:S(2)}) copy-start(s32[1,1,2048]{2,1,0:T(1,128)} %param.20) | copy-start | bytes 24580
  8.4 11.9 %copy-start.12 = (s32[1,1,4,2048]{3,2,1,0:T(4,128)S(1)}, s32[1,1,4,2048]{3,2,1,0:T(4,128)}, u32[]{:S(2)}) copy-start(s32[1,1,4,2048]{3,2,1,0:T(4,128)} %param.22) | copy-start | bytes 98308
  8.4 11.9 %copy-start.11 = (f32[1,1,4,2048]{3,2,1,0:T(4,128)S(1)}, f32[1,1,4,2048]{3,2,1,0:T(4,128)}, u32[]{:S(2)}) copy-start(f32[1,1,4,2048]{3,2,1,0:T(4,128)} %param.23) | copy-start | bytes 98308
  8.4 11.9 %copy-start.13 = (f32[1,1,2048]{2,1,0:T(1,128)S(1)}, f32[1,1,2048]{2,1,0:T(1,128)}, u32[]{:S(2)}) copy-start(f32[1,1,2048]{2,1,0:T(1,128)} %param.24) | copy-start | bytes 24580
  8.4 11.9 %copy-start.14 = (f32[1,1,2048]{2,1,0:T(1,128)S(1)}, f32[1,1,2048]{2,1,0:T(1,128)}, u32[]{:S(2)}) copy-start(f32[1,1,2048]{2,1,0:T(1,128)} %param.25) | copy-start | bytes 24580
  8.4 13.9 %copy-start.3 = (bf16[2,64,64]{2,1,0:T(8,128)(2,1)S(1)}, bf16[2,64,64]{2,1,0:T(8,128)(2,1)}, u32[]{:S(2)}) copy-start(bf16[2,64,64]{2,1,0:T(8,128)(2,1)} %map_ref.1) | copy-start | bytes 49156
  8.4 13.9 %copy-start.5 = (f32[4]{0:T(128)S(1)}, f32[4]{0:T(128)}, u32[]{:S(2)}) copy-start(f32[4]{0:T(128)} %param.14) | copy-start | bytes 52
  8.4 13.8 %copy-start.6 = (f32[4]{0:T(128)S(1)}, f32[4]{0:T(128)}, u32[]{:S(2)}) copy-start(f32[4]{0:T(128)} %param.15) | copy-start | bytes 52
  8.5 13.8 %copy-start.7 = (f32[4]{0:T(128)S(1)}, f32[4]{0:T(128)}, u32[]{:S(2)}) copy-start(f32[4]{0:T(128)} %param.16) | copy-start | bytes 52
  8.5 13.8 %copy-start.8 = (f32[4]{0:T(128)S(1)}, f32[4]{0:T(128)}, u32[]{:S(2)}) copy-start(f32[4]{0:T(128)} %param.17) | copy-start | bytes 52
  8.5 53.2 %all-to-all-start = ((bf16[64,16,1536]{2,1,0:T(8,128)(2,1)}), bf16[64,16,1536]{2,1,0:T(8,128)(2,1)S(1)}, u32[]{:S(2)}, u32[]{:S(2)}) async-start(bf16[64,16,1536]{2,1,0:T(8,128)(2,1)} %forward_zonal.1), calls=%async_computation | async-start | bytes 6291456 | tf_op jit(solution)/shard_map/all_to_all | solution.py:547
  20.1 1.2 collective-permute-start
  20.6 1.7 %collective-permute-start.1 = (f32[12,2048]{1,0:T(8,128)S(1)}, f32[12,2048]{1,0:T(8,128)S(1)}, u32[]{:S(2)}, u32[]{:S(2)}) collective-permute-start(f32[12,2048]{1,0:T(8,128)S(1)} %concatenate.3.mine_ref), channel_id=1, source_target_pairs={{0,1},{1,0},{2,3},{3,2},{4,5},{5,4},{6,7},{7,6},{8,9},{9,8},{10,11... | collective-permute-start | bytes 294920 | tf_op jit(solution)/shard_map/ppermute | solution.py:531
  33.7 2.7 %copy-start = (bf16[2,2048,768]{2,1,0:T(8,128)(2,1)}, bf16[2,2048,768]{2,1,0:T(8,128)(2,1)S(1)}, u32[]{:S(2)}) copy-start(bf16[2,2048,768]{2,1,0:T(8,128)(2,1)S(1)} %get-tuple-element.14.turned_hbm) | copy-start | bytes 18874372
  36.4 0.9 copy-start.1
  37.3 0.7 copy-start.2
  38.0 1.5 %copy-start.9 = (bf16[256,5376]{1,0:T(8,128)(2,1)}, bf16[256,5376]{1,0:T(8,128)(2,1)S(1)}, u32[]{:S(2)}) copy-start(bf16[256,5376]{1,0:T(8,128)(2,1)S(1)} %get-tuple-element.20.slab_hbm) | copy-start | bytes 8257540
  66.2 1.3 collective-permute-start.2
  70.7 48.7 %copy-start.10 = (bf16[256,5376]{1,0:T(8,128)(2,1)S(1)}, bf16[256,5376]{1,0:T(8,128)(2,1)}, u32[]{:S(2)}) copy-start(bf16[256,5376]{1,0:T(8,128)(2,1)} %copy-done.9) | copy-start | bytes 8257540
